TPU v7x, 32 devices: a whole 2x2x4 slice. The times are simulated.
32 devices in a mesh: pipe: 2 (over core), heads: 2 (over x), shard: 8 (over z, y).
Axes of the slice: x: 2, y: 2, z: 4, core: 2. Of those that a mesh axis runs over, the one named last changes fastest.
Arguments:
- inputs: bfloat16 [16, 256, 384], P('shard'), may hold values from -6 to 6
- conditioning: bfloat16 [16, 384], P('shard'), may hold values from -6 to 6
- out_grad: float32 [16, 256, 384], P('shard'), may hold values from -6 to 6
- weight_mod: bfloat16 [2, 384, 6, 384], P('pipe', 'shard'), may hold values from -0.3125 to 0.3125
- bias_mod: bfloat16 [2, 6, 384], P('pipe', None, 'shard'), may hold values from -1.796875 to 1.796875
- weight_qkv: bfloat16 [2, 384, 3, 384], P('pipe', 'shard', None, 'heads'), may hold values from -0.3125 to 0.3125
- bias_qv: bfloat16 [2, 2, 384], P('pipe', None, ('heads', 'shard')), may hold values from -3 to 3
- weight_out: bfloat16 [2, 384, 384], P('pipe', 'heads', 'shard'), may hold values from -3 to 3
- bias_out: bfloat16 [2, 384], P('pipe', 'shard'), may hold values from -1.796875 to 1.796875
- first_feed_weight: bfloat16 [2, 384, 1536], P('pipe', 'shard', 'heads'), may hold values from -0.3125 to 0.3125
- first_feed_bias: bfloat16 [2, 1536], P('pipe', ('heads', 'shard')), may hold values from -3 to 3
- second_feed_weight: bfloat16 [2, 1536, 384], P('pipe', 'heads', 'shard'), may hold values from -0.15625 to 0.15625
- second_feed_bias: bfloat16 [2, 384], P('pipe', 'shard'), may hold values from -1.796875 to 1.796875
Outputs:
- activations: bfloat16 [2, 16, 256, 384], P('pipe', 'shard')
- input_grads: float32 [2, 16, 256, 384], P('pipe', 'shard')
- cond_grad: float32 [16, 384], P('shard')
- grad_weight_mod: float32 [2, 384, 6, 384], P('pipe', 'shard')
- grad_bias_mod: float32 [2, 6, 384], P('pipe', None, 'shard')
- grad_weight_qkv: float32 [2, 384, 3, 384], P('pipe', 'shard', None, 'heads')
- grad_bias_qv: float32 [2, 2, 384], P('pipe', None, ('heads', 'shard'))
- grad_weight_out: float32 [2, 384, 384], P('pipe', 'heads', 'shard')
- grad_bias_out: float32 [2, 384], P('pipe', 'shard')
- grad_weight_up: float32 [2, 384, 1536], P('pipe', 'shard', 'heads')
- grad_bias_up: float32 [2, 1536], P('pipe', ('heads', 'shard'))
- grad_weight_down: float32 [2, 1536, 384], P('pipe', 'heads', 'shard')
- grad_bias_down: float32 [2, 384], P('pipe', 'shard')
All inputs are finite; a program needn't handle non-finite values.
Results may differ from a plain program's by a relative error of at most 0.024.
Values may be sent and summed in bfloat16 or wider, within the bound.
A program may use at most 128 MiB of HBM per device.

v0:
```python
from functools import partial

import jax
import jax.numpy as jnp
from jax import lax
from jax.sharding import PartitionSpec as P

HD = 64
MB = 2


def passed_along(value, axis, by):
    peers = lax.axis_size(axis)
    pairs = [(i, i + by) for i in range(peers) if 0 <= i + by < peers]
    return lax.ppermute(value, axis, pairs)


def in_blocks(value, dim, peers):
    before, after = (value.shape[:dim], value.shape[dim + 1 :])
    return jnp.moveaxis(value.reshape(*before, peers, -1, *after), dim, 0)


def sent_and_summed(value, axis, dim):
    tiles = in_blocks(value, dim, lax.axis_size(axis))
    arrived = lax.all_to_all(tiles, axis, split_axis=0, concat_axis=0, tiled=True)
    return arrived.astype(jnp.float32).sum(axis=0)


def in_one_piece(arrays, axis, dim, along):
    columns = [a.reshape(*a.shape[:along], -1) for a in arrays]
    both = jnp.concatenate(columns, axis=along)
    out, at, gathered = (sent_and_summed(both, axis, dim), 0, [])
    for a, column in zip(arrays, columns):
        section = out[..., at : at + column.shape[along]]
        gathered.append(section.reshape(*section.shape[:along], *a.shape[along:]))
        at += column.shape[along]
    return tuple(gathered)


def head_total(partial_sum):
    share = lax.psum_scatter(
        partial_sum.astype(jnp.bfloat16), "heads", scatter_dimension=1, tiled=True
    ).astype(jnp.float32)
    return lax.all_gather(share.astype(jnp.bfloat16), "heads", axis=1, tiled=True).astype(
        share.dtype
    )


def norm_rows(values):
    average = jnp.mean(values, axis=-1, keepdims=True)
    centered = values - average
    variance = jnp.mean(centered * centered, axis=-1, keepdims=True)
    inverse = lax.rsqrt(variance + 1e-06)
    return (centered * inverse, inverse)


def norm_back(grad_norm, normed, inverse):
    return inverse * (
        grad_norm
        - jnp.mean(grad_norm, axis=-1, keepdims=True)
        - normed * jnp.mean(grad_norm * normed, axis=-1, keepdims=True)
    )


def token_sum(values):
    return jnp.sum(values, axis=1)


def forward_pass(entering, condition, weights):
    (
        weight_mod,
        bias_mod,
        weight_qkv,
        bias_qv,
        weight_out,
        bias_out,
        first_feed_weight,
        first_feed_bias,
        second_feed_weight,
        second_feed_bias,
    ) = weights
    latents, length, model_width = entering.shape
    local_width = weight_qkv.shape[2]
    state_in = entering.astype(jnp.float32)
    cond_full = condition.astype(jnp.float32)
    cond_act = jax.nn.silu(cond_full).astype(jnp.bfloat16)
    modulation = jnp.einsum(
        "ld,dke->lke", cond_act, weight_mod, preferred_element_type=jnp.float32
    ) + bias_mod.astype(jnp.float32)
    mod_rows = [modulation[:, column][:, None, :] for column in range(6)]
    norm_one, inverse_one = norm_rows(state_in)
    normed = (norm_one * (1.0 + mod_rows[1]) + mod_rows[0]).astype(jnp.bfloat16)
    projected = jnp.einsum("lsd,dke->lske", normed, weight_qkv, preferred_element_type=jnp.float32)
    biases = bias_qv.astype(jnp.float32)
    query_heads = (
        (projected[:, :, 0] + biases[0]).astype(jnp.bfloat16).reshape(latents, length, -1, HD)
    )
    key_heads = projected[:, :, 1].astype(jnp.bfloat16).reshape(latents, length, -1, HD)
    value_heads = (
        (projected[:, :, 2] + biases[1]).astype(jnp.bfloat16).reshape(latents, length, -1, HD)
    )
    scores = jnp.einsum(
        "lqhe,lkhe->lhqk", query_heads, key_heads, preferred_element_type=jnp.float32
    ) * HD ** (-0.5)
    highest_score = jnp.max(scores, axis=-1, keepdims=True)
    expo_scores = jnp.exp(scores - highest_score)
    score_total = jnp.sum(expo_scores, axis=-1, keepdims=True)
    attn_probs = expo_scores / score_total
    log_total = highest_score + jnp.log(score_total)
    mixed_heads = jnp.einsum(
        "lhqk,lkhe->lqhe",
        attn_probs.astype(jnp.bfloat16),
        value_heads,
        preferred_element_type=jnp.float32,
    )
    mixed_heads = mixed_heads.reshape(latents, length, local_width).astype(jnp.bfloat16)
    attended = head_total(
        jnp.einsum("lse,ed->lsd", mixed_heads, weight_out, preferred_element_type=jnp.float32)
    ) + bias_out.astype(jnp.float32)
    hidden = state_in + mod_rows[2] * attended
    norm_two, inverse_two = norm_rows(hidden)
    second_normalized = (norm_two * (1.0 + mod_rows[4]) + mod_rows[3]).astype(jnp.bfloat16)
    raised_hidden = jnp.einsum(
        "ikx,xc->ikc", second_normalized, first_feed_weight, preferred_element_type=jnp.float32
    ) + first_feed_bias.astype(jnp.float32)
    hidden_activated = jax.nn.gelu(raised_hidden, approximate=True).astype(jnp.bfloat16)
    lowered_output = head_total(
        jnp.einsum(
            "vua,ap->vup", hidden_activated, second_feed_weight, preferred_element_type=jnp.float32
        )
    ) + second_feed_bias.astype(jnp.float32)
    result = hidden + mod_rows[5] * lowered_output
    kept_state = (
        cond_full,
        cond_act,
        mod_rows,
        norm_one,
        inverse_one,
        normed,
        query_heads,
        key_heads,
        value_heads,
        log_total,
        mixed_heads,
        attended,
        norm_two,
        inverse_two,
        second_normalized,
        raised_hidden,
        hidden_activated,
        lowered_output,
    )
    return (result, kept_state)


def backward_pass(grad_out, kept_state, weights):
    (
        weight_mod,
        bias_mod,
        weight_qkv,
        bias_qv,
        weight_out,
        bias_out,
        first_feed_weight,
        first_feed_bias,
        second_feed_weight,
        second_feed_bias,
    ) = weights
    (
        cond_full,
        cond_act,
        mod_rows,
        norm_one,
        inverse_one,
        normed,
        query_heads,
        key_heads,
        value_heads,
        log_total,
        mixed_heads,
        attended,
        norm_two,
        inverse_two,
        second_normalized,
        raised_hidden,
        hidden_activated,
        lowered_output,
    ) = kept_state
    latents, length, model_width = grad_out.shape
    local_width = mixed_heads.shape[2]
    lower_projection_gradient = (mod_rows[5] * grad_out).astype(jnp.bfloat16)
    grad_gate_two = token_sum(grad_out * lowered_output)
    gradient_lower_weight = jnp.einsum(
        "prb,pry->by",
        hidden_activated,
        lower_projection_gradient,
        preferred_element_type=jnp.float32,
    )
    grad_bias_down = jnp.sum(lower_projection_gradient.astype(jnp.float32), axis=(0, 1))
    activation_gradient = jnp.einsum(
        "hot,jt->hoj",
        lower_projection_gradient,
        second_feed_weight,
        preferred_element_type=jnp.float32,
    )
    raise_projection_gradient = jax.vjp(partial(jax.nn.gelu, approximate=True), raised_hidden)[1](
        activation_gradient
    )[0].astype(jnp.bfloat16)
    gradient_raise_weight = jnp.einsum(
        "hrp,hrt->pt",
        second_normalized,
        raise_projection_gradient,
        preferred_element_type=jnp.float32,
    )
    grad_bias_up = jnp.sum(raise_projection_gradient.astype(jnp.float32), axis=(0, 1))
    normed_two_grad = head_total(
        jnp.einsum(
            "twe,ue->twu",
            raise_projection_gradient,
            first_feed_weight,
            preferred_element_type=jnp.float32,
        )
    )
    grad_scale_two = token_sum(normed_two_grad * norm_two)
    grad_shift_two = token_sum(normed_two_grad)
    hidden_grad = grad_out + norm_back(normed_two_grad * (1.0 + mod_rows[4]), norm_two, inverse_two)
    attend_grad = (mod_rows[2] * hidden_grad).astype(jnp.bfloat16)
    grad_gate_one = token_sum(hidden_grad * attended)
    grad_out_proj = jnp.einsum(
        "lse,lsd->ed", mixed_heads, attend_grad, preferred_element_type=jnp.float32
    )
    grad_bias_out = jnp.sum(attend_grad.astype(jnp.float32), axis=(0, 1))
    mixed_grad = jnp.einsum(
        "lsd,ed->lse", attend_grad, weight_out, preferred_element_type=jnp.float32
    )
    mixed_grad = mixed_grad.astype(jnp.bfloat16).reshape(latents, length, -1, HD)
    scaling = HD ** (-0.5)
    scores = (
        jnp.einsum("lqhe,lkhe->lhqk", query_heads, key_heads, preferred_element_type=jnp.float32)
        * scaling
    )
    attn_probs = jnp.exp(scores - log_total)
    value_grad = jnp.einsum(
        "lhqk,lqhe->lkhe",
        attn_probs.astype(jnp.bfloat16),
        mixed_grad,
        preferred_element_type=jnp.float32,
    )
    prob_grad = jnp.einsum(
        "lqhe,lkhe->lhqk", mixed_grad, value_heads, preferred_element_type=jnp.float32
    )
    score_grad = (
        attn_probs * (prob_grad - jnp.sum(attn_probs * prob_grad, axis=-1, keepdims=True))
    ).astype(jnp.bfloat16)
    query_grad = (
        jnp.einsum("lhqk,lkhe->lqhe", score_grad, key_heads, preferred_element_type=jnp.float32)
        * scaling
    )
    key_grad = (
        jnp.einsum("lhqk,lqhe->lkhe", score_grad, query_heads, preferred_element_type=jnp.float32)
        * scaling
    )
    proj_grad = (
        jnp.stack([query_grad, key_grad, value_grad], axis=2)
        .reshape(latents, length, 3, local_width)
        .astype(jnp.bfloat16)
    )
    grad_qkv = jnp.einsum("lsd,lske->dke", normed, proj_grad, preferred_element_type=jnp.float32)
    proj_sums = jnp.sum(proj_grad.astype(jnp.float32), axis=(0, 1))
    grad_bias_qv = jnp.stack([proj_sums[0], proj_sums[2]])
    normed_grad = head_total(
        jnp.einsum("lske,dke->lsd", proj_grad, weight_qkv, preferred_element_type=jnp.float32)
    )
    grad_scale_one = token_sum(normed_grad * norm_one)
    grad_shift_one = token_sum(normed_grad)
    input_grad = hidden_grad + norm_back(normed_grad * (1.0 + mod_rows[1]), norm_one, inverse_one)
    mod_grad = jnp.stack(
        [
            grad_shift_one,
            grad_scale_one,
            grad_gate_one,
            grad_shift_two,
            grad_scale_two,
            grad_gate_two,
        ],
        axis=1,
    ).astype(jnp.bfloat16)
    grad_mod = jnp.einsum("ld,lke->dke", cond_act, mod_grad, preferred_element_type=jnp.float32)
    grad_bias_mod = jnp.sum(mod_grad.astype(jnp.float32), axis=0)
    silu_grad = jnp.einsum("lke,dke->ld", mod_grad, weight_mod, preferred_element_type=jnp.float32)
    cond_grad = jax.vjp(jax.nn.silu, cond_full)[1](silu_grad)[0]
    grads = (
        grad_mod,
        grad_bias_mod,
        grad_qkv,
        grad_bias_qv,
        grad_out_proj,
        grad_bias_out,
        gradient_raise_weight,
        grad_bias_up,
        gradient_lower_weight,
        grad_bias_down,
    )
    return (grads, input_grad, cond_grad, cond_act, mod_grad)


def per_device(
    inputs,
    conditioning,
    out_grad,
    weight_mod,
    bias_mod,
    weight_qkv,
    bias_qv,
    weight_out,
    bias_out,
    first_feed_weight,
    first_feed_bias,
    second_feed_weight,
    second_feed_bias,
):
    gathered = (
        lax.all_gather(weight_mod, "shard", axis=1, tiled=True),
        lax.all_gather(bias_mod, "shard", axis=2, tiled=True),
        lax.all_gather(weight_qkv, "shard", axis=1, tiled=True),
        lax.all_gather(bias_qv, "shard", axis=2, tiled=True),
        lax.all_gather(weight_out, "shard", axis=2, tiled=True),
        lax.all_gather(bias_out, "shard", axis=1, tiled=True),
        lax.all_gather(first_feed_weight, "shard", axis=1, tiled=True),
        lax.all_gather(first_feed_bias, "shard", axis=1, tiled=True),
        lax.all_gather(second_feed_weight, "shard", axis=2, tiled=True),
        lax.all_gather(second_feed_bias, "shard", axis=1, tiled=True),
    )
    weights = tuple((matrix[0] for matrix in gathered))
    section_index = lax.axis_index("pipe")
    leading = section_index == 0
    batches = MB
    latents_dev, length, model_width = inputs.shape
    batch_size = latents_dev // batches
    input_batches = inputs.reshape(batches, batch_size, length, model_width)
    cond_batches = conditioning.reshape(batches, batch_size, model_width)
    grad_batches = out_grad.reshape(batches, batch_size, length, model_width)
    received = jnp.zeros((batch_size, length, model_width), jnp.bfloat16)
    sent_list = []
    kept_list = []
    for tick in range(batches + 1):
        batch_index = jnp.clip(tick - section_index, 0, batches - 1)
        fresh = lax.dynamic_index_in_dim(input_batches, batch_index, 0, keepdims=False)
        condition = lax.dynamic_index_in_dim(cond_batches, batch_index, 0, keepdims=False)
        entering = jnp.where(leading, fresh, received)
        result, kept_state = forward_pass(entering, condition, weights)
        sending = result.astype(jnp.bfloat16)
        sent_list.append(sending)
        kept_list.append(kept_state)
        if tick < batches:
            received = passed_along(sending, "pipe", 1)
    activations = jnp.stack(
        [jnp.where(leading, sent_list[batch], sent_list[batch + 1]) for batch in range(batches)]
    )
    activations = activations.reshape(1, latents_dev, length, model_width)
    back_received = jnp.zeros((batch_size, length, model_width), jnp.bfloat16)
    input_list = []
    cond_list = []
    factor_cond = []
    factor_mod = []
    totals = None
    mod_sums = None
    for tick in range(batches + 1):
        kept_state = kept_list[batches - tick]
        upstream = grad_batches[max(batches - 1 - tick, 0)]
        valid = jnp.where(leading, tick >= 1, tick <= batches - 1)
        grad_in = jnp.where(leading, back_received.astype(jnp.float32), upstream)
        grad_in = jnp.where(valid, grad_in, jnp.zeros_like(grad_in))
        grads, input_grad, cond_grad, cond_act, mod_grad = backward_pass(
            grad_in, kept_state, weights
        )
        input_list.append(input_grad)
        cond_list.append(cond_grad)
        factor_cond.append(cond_act)
        factor_mod.append(mod_grad)
        mod_pair = (grads[0], grads[1])
        mod_sums = mod_pair if mod_sums is None else jax.tree.map(jnp.add, mod_sums, mod_pair)
        shares = (
            sent_and_summed(grads[2][None].astype(jnp.bfloat16), "shard", 1),
            sent_and_summed(grads[3][None].astype(jnp.bfloat16), "shard", 2),
            sent_and_summed(grads[4][None].astype(jnp.bfloat16), "shard", 2),
            *in_one_piece(
                (grads[5][None].astype(jnp.bfloat16), grads[6][None].astype(jnp.bfloat16)),
                "shard",
                1,
                2,
            ),
            sent_and_summed(grads[7][None].astype(jnp.bfloat16), "shard", 1),
            sent_and_summed(grads[8][None].astype(jnp.bfloat16), "shard", 2),
            sent_and_summed(grads[9][None].astype(jnp.bfloat16), "shard", 1),
        )
        totals = shares if totals is None else jax.tree.map(jnp.add, totals, shares)
        if tick < batches:
            back_received = passed_along(input_grad.astype(jnp.bfloat16), "pipe", -1)
    grad_mod_own, grad_bias_own = (
        sent_and_summed(mod_sums[0][None].astype(jnp.bfloat16), "shard", 1),
        sent_and_summed(mod_sums[1][None].astype(jnp.bfloat16), "shard", 2),
    )
    input_grads = jnp.stack(
        [
            jnp.where(leading, input_list[batches - batch], input_list[batches - 1 - batch])
            for batch in range(batches)
        ]
    )
    input_grads = input_grads.reshape(1, latents_dev, length, model_width)
    cond_local = jnp.stack(
        [
            jnp.where(leading, cond_list[batches - batch], cond_list[batches - 1 - batch])
            for batch in range(batches)
        ]
    )
    cond_total = lax.psum(cond_local.reshape(latents_dev, model_width), "pipe")
    return (activations, input_grads, cond_total, grad_mod_own, grad_bias_own) + tuple(totals)


def solution(mesh):
    return jax.shard_map(
        per_device,
        mesh=mesh,
        in_specs=(
            P("shard", None, None),
            P("shard", None),
            P("shard", None, None),
            P("pipe", "shard", None, None),
            P("pipe", None, "shard"),
            P("pipe", "shard", None, "heads"),
            P("pipe", None, ("heads", "shard")),
            P("pipe", "heads", "shard"),
            P("pipe", "shard"),
            P("pipe", "shard", "heads"),
            P("pipe", ("heads", "shard")),
            P("pipe", "heads", "shard"),
            P("pipe", "shard"),
        ),
        out_specs=(
            P("pipe", "shard", None, None),
            P("pipe", "shard", None, None),
            P("shard", None),
            P("pipe", "shard", None, None),
            P("pipe", None, "shard"),
            P("pipe", "shard", None, "heads"),
            P("pipe", None, ("heads", "shard")),
            P("pipe", "heads", "shard"),
            P("pipe", "shard"),
            P("pipe", "shard", "heads"),
            P("pipe", ("heads", "shard")),
            P("pipe", "heads", "shard"),
            P("pipe", "shard"),
        ),
        check_vma=False,
    )
```

profile of v0, /device:TPU:0, one launch (start us, length us, event | category | flops | bytes accessed | tf_op | source)
XLA Modules:
  0.0 846.0 jit_solution(15871365522495800447)
XLA Ops:
  13.1 23.7 %all-reduce.3 = (bf16[768]{0:T(1024)(128)(2,1)S(1)}, bf16[384]{0:T(512)(128)(2,1)S(1)}, bf16[384]{0:T(512)(128)(2,1)}) all-reduce(bf16[768]{0:T(1024)(128)(2,1)S(1)} %dynamic-update-slice.1, bf16[384]{0:T(512)(128)(2,1)S(1)} %dynamic-update-slice, ...), channel_id=1, replica_groups=mesh['pipe'=2,'heads'=2,'shard'=8] {'shard'}, use_global_device_ids=true, to_apply=%add.1 | all-reduce | flops 1536 | bytes 6144
  38.9 30.9 %all_gather.69 = bf16[1,2,192]{1,0,2:T(2,128)(2,1)S(1)} all-gather(bf16[1,2,24]{1,0,2:T(2,128)(2,1)S(1)} %copy.105), channel_id=1, replica_groups=mesh['pipe'=2,'heads'=2,'shard'=8] {'shard'}, dimensions={2}, use_global_device_ids=true | all-gather | bytes 864 | tf_op jit(solution)/shard_map/all_gather | solution.py:326
  73.7 30.8 %all_gather.67 = bf16[1,6,384]{1,0,2:T(2,128)(2,1)S(1)} all-gather(bf16[1,6,48]{1,0,2:T(2,128)(2,1)S(1)} %copy.103), channel_id=1, replica_groups=mesh['pipe'=2,'heads'=2,'shard'=8] {'shard'}, dimensions={2}, use_global_device_ids=true | all-gather | bytes 5184 | tf_op jit(solution)/shard_map/all_gather | solution.py:324
  104.7 31.5 %all_gather.68 = bf16[1,384,3,192]{3,1,2,0:T(8,128)(2,1)S(1)} all-gather(bf16[1,48,3,192]{3,1,2,0:T(8,128)(2,1)} %param.18), channel_id=1, replica_groups=mesh['pipe'=2,'heads'=2,'shard'=8] {'shard'}, dimensions={1}, use_global_device_ids=true | all-gather | bytes 497664 | tf_op jit(solution)/shard_map/all_gather | solution.py:325
  136.6 30.7 %all_gather.70 = bf16[1,192,384]{1,2,0:T(8,128)(2,1)S(1)} all-gather(bf16[1,192,48]{1,2,0:T(8,128)(2,1)S(1)} %copy-done.132), channel_id=1, replica_groups=mesh['pipe'=2,'heads'=2,'shard'=8] {'shard'}, dimensions={2}, use_global_device_ids=true | all-gather | bytes 165888 | tf_op jit(solution)/shard_map/all_gather | solution.py:327
  178.4 33.5 %all_gather.73 = bf16[1,384,768]{2,1,0:T(8,128)(2,1)} all-gather(bf16[1,48,768]{2,1,0:T(8,128)(2,1)S(1)} %copy-done.99), channel_id=1, replica_groups=mesh['pipe'=2,'heads'=2,'shard'=8] {'shard'}, dimensions={1}, use_global_device_ids=true | all-gather | bytes 663552 | tf_op jit(solution)/shard_map/all_gather | solution.py:329
  211.9 33.5 %all_gather.75 = bf16[1,768,384]{1,2,0:T(8,128)(2,1)} all-gather(bf16[1,768,48]{1,2,0:T(8,128)(2,1)} %param.24), channel_id=1, replica_groups=mesh['pipe'=2,'heads'=2,'shard'=8] {'shard'}, dimensions={2}, use_global_device_ids=true | all-gather | bytes 663552 | tf_op jit(solution)/shard_map/all_gather | solution.py:331
  255.1 8.2 reduce-scatter.15.cloned.1.call-done
  275.9 11.1 %reduce-scatter.17.cloned.1.call-done = bf16[1,128,384]{2,1,0:T(8,128)(2,1)} async-done(((bf16[1,256,384]{2,1,0:T(8,128)(2,1)}), bf16[1,128,384]{2,1,0:T(8,128)(2,1)}) %reduce-scatter.17.cloned.1.call-update) | async-done | bytes 98320 | tf_op jit(solution)/shard_map/reduce_scatter | solution.py:41
  286.9 5.8 all_gather.78
  334.1 9.5 %reduce-scatter.21.cloned.1.call-done = bf16[1,128,384]{2,1,0:T(8,128)(2,1)} async-done(((bf16[1,256,384]{2,1,0:T(8,128)(2,1)}), bf16[1,128,384]{2,1,0:T(8,128)(2,1)}) %reduce-scatter.21.cloned.1.call-update) | async-done | bytes 98320 | tf_op jit(solution)/shard_map/reduce_scatter | solution.py:41
  372.1 6.5 reduce-scatter.25.cloned.1.call-done
  443.1 5.7 all_gather.83
  507.7 6.5 all-to-all-done.8
  555.3 5.9 all-to-all-start.2
  583.4 6.5 all_gather.86
  589.8 6.2 all-to-all-start.11
  601.9 12.4 %all-to-all-done.11 = bf16[8,1,48,769]{3,2,1,0:T(8,128)(2,1)} async-done(((bf16[8,1,48,769]{3,2,1,0:T(8,128)(2,1)}), bf16[8,1,48,769]{3,2,1,0:T(8,128)(2,1)}, u32[]{:S(2)}, u32[]{:S(2)}) %all-to-all-start.11) | async-done | bytes 590624 | tf_op jit(solution)/shard_map/all_to_all | solution.py:25
  668.6 5.9 all-to-all-start.3
  721.6 5.7 all-to-all-done.10
  755.9 5.9 all-to-all-start.4
  774.9 6.0 all-to-all-start.13
  787.8 6.2 all-to-all-done.13
  814.3 22.2 %all-to-all-done = bf16[8,1,48,6,384]{4,2,3,1,0:T(8,128)(2,1)} async-done(((bf16[8,1,48,6,384]{4,2,3,1,0:T(8,128)(2,1)}), bf16[8,1,48,6,384]{4,2,3,1,0:T(8,128)(2,1)}, u32[]{:S(2)}, u32[]{:S(2)}) %all-to-all-start) | async-done | bytes 1769504 | tf_op jit(solution)/shard_map/all_to_all | solution.py:25
  (813 shorter events, 477.0 us)
Async XLA Ops:
  7.2 160.4 %all-gather.2.cloned.1.call-start = ((), (), s32[]{:S(2)}) async-start(), calls=%async_computation.35 | async-start | bytes 1990656 | tf_op jit(solution)/shard_map/all_gather | solution.py:323
  7.9 237.5 %reduce-scatter.13.cloned.1.call-start = ((), (), s32[]{:S(2)}) async-start(), calls=%async_computation.36 | async-start | bytes 294912 | tf_op jit(solution)/shard_map/reduce_scatter | solution.py:41
  178.4 85.0 %reduce-scatter.15.cloned.1.call-start = ((), (), s32[]{:S(2)}) async-start(), calls=%async_computation.37 | async-start | bytes 294912 | tf_op jit(solution)/shard_map/reduce_scatter | solution.py:41
  255.0 31.9 %reduce-scatter.17.cloned.1.call-start = ((), (), s32[]{:S(2)}) async-start(), calls=%async_computation.38 | async-start | bytes 294912 | tf_op jit(solution)/shard_map/reduce_scatter | solution.py:41
  275.8 37.8 %reduce-scatter.19.cloned.1.call-start = ((), (), s32[]{:S(2)}) async-start(), calls=%async_computation.39 | async-start | bytes 294912 | tf_op jit(solution)/shard_map/reduce_scatter | solution.py:41
  308.0 17.1 %all-to-all-start.20 = ((bf16[8,1,48]{2,1,0:T(2,128)(2,1)}), bf16[8,1,48]{2,1,0:T(2,128)(2,1)}, u32[]{:S(2)}, u32[]{:S(2)}) async-start(bf16[8,1,48]{2,1,0:T(2,128)(2,1)} %convert_element_type.1143), calls=%async_computation.32 | async-start | bytes 8192 | tf_op jit(solution)/shard_map/all_to_all | solution.py:25
  313.6 30.0 %reduce-scatter.21.cloned.1.call-start = ((), (), s32[]{:S(2)}) async-start(), calls=%async_computation.40 | async-start | bytes 294912 | tf_op jit(solution)/shard_map/reduce_scatter | solution.py:41
  363.5 15.1 %reduce-scatter.25.cloned.1.call-start = ((), (), s32[]{:S(2)}) async-start(), calls=%async_computation.42 | async-start | bytes 294912 | tf_op jit(solution)/shard_map/reduce_scatter | solution.py:41
  365.9 26.0 %reduce-scatter.23.cloned.1.call-start = ((), (), s32[]{:S(2)}) async-start(), calls=%async_computation.41 | async-start | bytes 294912 | tf_op jit(solution)/shard_map/reduce_scatter | solution.py:41
  423.0 77.5 %all-to-all-start.5 = ((bf16[8,1,2,24]{3,2,1,0:T(2,128)(2,1)}), bf16[8,1,2,24]{3,2,1,0:T(2,128)(2,1)}, u32[]{:S(2)}, u32[]{:S(2)}) async-start(bf16[8,1,2,24]{3,2,1,0:T(2,128)(2,1)} %copy.126), calls=%async_computation.17 | async-start | bytes 8192 | tf_op jit(solution)/shard_map/all_to_all | solution.py:25
  429.3 50.5 %reduce-scatter.29.cloned.1.call-start = ((), (), s32[]{:S(2)}) async-start(), calls=%async_computation.44 | async-start | bytes 294912 | tf_op jit(solution)/shard_map/reduce_scatter | solution.py:41
  468.5 48.9 %reduce-scatter.31.cloned.1.call-start = ((), (), s32[]{:S(2)}) async-start(), calls=%async_computation.45 | async-start | bytes 294912 | tf_op jit(solution)/shard_map/reduce_scatter | solution.py:41
  535.3 20.0 %all-to-all-start.17 = ((bf16[8,1,768,48]{2,3,1,0:T(8,128)(2,1)}), bf16[8,1,768,48]{2,3,1,0:T(8,128)(2,1)}, u32[]{:S(2)}, u32[]{:S(2)}) async-start(bf16[8,1,768,48]{2,3,1,0:T(8,128)(2,1)} %bitcast.525), calls=%async_computation.29 | async-start | bytes 1179648 | tf_op jit(solution)/shard_map/all_to_all | solution.py:25
  555.3 22.9 %all-to-all-start.2 = ((bf16[8,1,48,3,192]{4,2,3,1,0:T(8,128)(2,1)}), bf16[8,1,48,3,192]{4,2,3,1,0:T(8,128)(2,1)}, u32[]{:S(2)}, u32[]{:S(2)}) async-start(bf16[8,1,48,3,192]{4,2,3,1,0:T(8,128)(2,1)} %copy.121), calls=%async_computation.14 | async-start | bytes 1179648 | tf_op jit(solution)/shard_map/all_to_all | solution.py:25
  561.2 22.1 %reduce-scatter.33.cloned.1.call-start = ((), (), s32[]{:S(2)}) async-start(), calls=%async_computation.46 | async-start | bytes 294912 | tf_op jit(solution)/shard_map/reduce_scatter | solution.py:41
  589.8 24.5 %all-to-all-start.11 = ((bf16[8,1,48,769]{3,2,1,0:T(8,128)(2,1)}), bf16[8,1,48,769]{3,2,1,0:T(8,128)(2,1)}, u32[]{:S(2)}, u32[]{:S(2)}) async-start(bf16[8,1,48,769]{3,2,1,0:T(8,128)(2,1)} %pad_maximum_fusion), calls=%async_computation.23 | async-start | bytes 1376256 | tf_op jit(solution)/shard_map/all_to_all | solution.py:25
  646.9 21.8 %all-to-all-start.18 = ((bf16[8,1,768,48]{2,3,1,0:T(8,128)(2,1)}), bf16[8,1,768,48]{2,3,1,0:T(8,128)(2,1)}, u32[]{:S(2)}, u32[]{:S(2)}) async-start(bf16[8,1,768,48]{2,3,1,0:T(8,128)(2,1)} %bitcast.526), calls=%async_computation.30 | async-start | bytes 1179648 | tf_op jit(solution)/shard_map/all_to_all | solution.py:25
  651.1 27.5 %reduce-scatter.35.cloned.1.call-start = ((), (), s32[]{:S(2)}) async-start(), calls=%async_computation.47 | async-start | bytes 294912 | tf_op jit(solution)/shard_map/reduce_scatter | solution.py:41
  668.6 18.0 %all-to-all-start.3 = ((bf16[8,1,48,3,192]{4,2,3,1,0:T(8,128)(2,1)}), bf16[8,1,48,3,192]{4,2,3,1,0:T(8,128)(2,1)S(1)}, u32[]{:S(2)}, u32[]{:S(2)}) async-start(bf16[8,1,48,3,192]{4,2,3,1,0:T(8,128)(2,1)} %copy.123), calls=%async_computation.15 | async-start | bytes 1179648 | tf_op jit(solution)/shard_map/all_to_all | solution.py:25
  696.7 19.1 %all-to-all-start.12 = ((bf16[8,1,48,769]{3,2,1,0:T(8,128)(2,1)}), bf16[8,1,48,769]{3,2,1,0:T(8,128)(2,1)}, u32[]{:S(2)}, u32[]{:S(2)}) async-start(bf16[8,1,48,769]{3,2,1,0:T(8,128)(2,1)} %pad_maximum_fusion.1), calls=%async_computation.24 | async-start | bytes 1376256 | tf_op jit(solution)/shard_map/all_to_all | solution.py:25
  737.1 18.8 %all-to-all-start.19 = ((bf16[8,1,768,48]{2,3,1,0:T(8,128)(2,1)}), bf16[8,1,768,48]{2,3,1,0:T(8,128)(2,1)S(1)}, u32[]{:S(2)}, u32[]{:S(2)}) async-start(bf16[8,1,768,48]{2,3,1,0:T(8,128)(2,1)} %bitcast.527), calls=%async_computation.31 | async-start | bytes 1179648 | tf_op jit(solution)/shard_map/all_to_all | solution.py:25
  755.9 19.0 %all-to-all-start.4 = ((bf16[8,1,48,3,192]{4,2,3,1,0:T(8,128)(2,1)}), bf16[8,1,48,3,192]{4,2,3,1,0:T(8,128)(2,1)}, u32[]{:S(2)}, u32[]{:S(2)}) async-start(bf16[8,1,48,3,192]{4,2,3,1,0:T(8,128)(2,1)} %copy.125), calls=%async_computation.16 | async-start | bytes 1179648 | tf_op jit(solution)/shard_map/all_to_all | solution.py:25
  774.9 19.1 %all-to-all-start.13 = ((bf16[8,1,48,769]{3,2,1,0:T(8,128)(2,1)}), bf16[8,1,48,769]{3,2,1,0:T(8,128)(2,1)S(1)}, u32[]{:S(2)}, u32[]{:S(2)}) async-start(bf16[8,1,48,769]{3,2,1,0:T(8,128)(2,1)} %pad_maximum_fusion.2), calls=%async_computation.25 | async-start | bytes 1376256 | tf_op jit(solution)/shard_map/all_to_all | solution.py:25
  794.0 42.5 %all-to-all-start = ((bf16[8,1,48,6,384]{4,2,3,1,0:T(8,128)(2,1)}), bf16[8,1,48,6,384]{4,2,3,1,0:T(8,128)(2,1)}, u32[]{:S(2)}, u32[]{:S(2)}) async-start(bf16[8,1,48,6,384]{4,2,3,1,0:T(8,128)(2,1)} %copy.118), calls=%async_computation.12 | async-start | bytes 3538944 | tf_op jit(solution)/shard_map/all_to_all | solution.py:25
  (223 other events, 2597.4 us)
Sparse Core Ops, SparseCore 0:
  10.3 49.8 all-gather.1
  178.5 8.1 reduce-scatter.12
  255.1 8.1 reduce-scatter.14
  275.9 10.9 reduce-scatter.16
  298.7 10.9 reduce-scatter.18
  332.2 11.3 reduce-scatter.20
  367.2 11.3 reduce-scatter.24
  380.8 10.9 reduce-scatter.22
  431.6 11.3 reduce-scatter.26
  468.6 11.0 reduce-scatter.28
  495.2 10.9 reduce-scatter.30
  565.9 12.2 reduce-scatter.32
  664.9 12.2 reduce-scatter.34
where the time goes:
time: 859 us; the launch traced here: 846 us
  blocking collectives  286 us (33%)
  waiting for transfers between devices  137 us (16%)
  other arithmetic  116 us (14%)
  starting transfers between devices  115 us (13%)
  local copies, waits for them, and re-layouts  104 us (12%)
  matrix products  69.5 us (8%)
  between operations  18.2 us (2%)
    all_to_all x23, starting transfers between devices, sent_and_summed(): lax.all_to_all(tiles, axis, split_axis=0, concat_axis=0, tiled=True)  109 us
    all_to_all x23, waiting for transfers between devices, sent_and_summed(): lax.all_to_all(tiles, axis, split_axis=0, concat_axis=0, tiled=True)  90.3 us
    all_gather x12, blocking collectives, head_total(): lax.all_gather(share.astype(jnp.bfloat16), 'heads', axis=1, tiled=True)  67.9 us
    reduce_scatter x12, waiting for transfers between devices, head_total(): lax.psum_scatter(partial_sum.astype(jnp.bfloat16), 'heads', scatter_dimen...  44.6 us
    all_gather x1, blocking collectives, per_device(): lax.all_gather(first_feed_weight, 'shard', axis=1, tiled=True)  33.5 us
    all_gather x1, blocking collectives, per_device(): lax.all_gather(second_feed_weight, 'shard', axis=2, tiled=True)  33.5 us
    all_gather x1, blocking collectives, per_device(): lax.all_gather(weight_qkv, 'shard', axis=1, tiled=True)  31.5 us
    unnamed x440, local copies, waits for them, and re-layouts  30.9 us
  transfers between devices with their start and end apart: 40, of which 23 were waited for; matrix products, arithmetic and copies ran while one was open for 26% of the time, Pallas kernels for 0%

commit v1 on v0

v1 whole, which is shorter than its diff:
```python
import math

import jax
import jax.numpy as jnp
from jax import lax
from jax.experimental import pallas as pl
from jax.experimental.pallas import tpu as pltpu
from jax.sharding import PartitionSpec as P

HD = 64
D = 384
EH = 192
FH = 768
QKV = 3 * EH
COLS = QKV + EH + 2 * FH
MODH = 3 * D
PAD = 128
WIDE = COLS + MODH + PAD
BIAS_COLS = 11
SCALING = HD**-0.5
SMALL = 6 * D + 2 * QKV + D + 2 * FH + D + D + D
BF = jnp.bfloat16
F32 = jnp.float32


def dot_nn(a, b):
    return lax.dot_general(a, b, (((1,), (0,)), ((), ())), preferred_element_type=F32)


def dot_nt(a, b):
    return lax.dot_general(a, b, (((1,), (1,)), ((), ())), preferred_element_type=F32)


def dot_tn(a, b):
    return lax.dot_general(a, b, (((0,), (0,)), ((), ())), preferred_element_type=F32)


def rows_mean(v):
    return jnp.mean(v, axis=-1, keepdims=True)


def norm_rows(v):
    centered = v - rows_mean(v)
    inverse = lax.rsqrt(rows_mean(centered * centered) + 1e-06)
    return centered * inverse, inverse


def norm_back(e, normed, inverse):
    return inverse * (e - rows_mean(e) - normed * rows_mean(e * normed))


def token_sum(v):
    return jnp.sum(v, axis=0, keepdims=True)


def block_kernel(
    latents,
    place,
    x_ref,
    cond_ref,
    g_ref,
    w_ref,
    bm_ref,
    bqkv_ref,
    bo_ref,
    bu_ref,
    bd_ref,
    act_out,
    grad_out,
    dw_out,
    small_out,
    n1_s,
    inv1_s,
    normed_s,
    qkv_s,
    probs_s,
    mixed_s,
    attended_s,
    n2_s,
    inv2_s,
    normed_two_s,
    slope_s,
    activated_s,
    down_s,
    mod_s,
    upg_s,
    pjg_s,
    back_s,
    dw_s,
):
    section = place[0]
    cond = cond_ref[0]
    sig = jax.nn.sigmoid(cond)
    cond_act = (cond * sig).astype(BF)
    cond_rows = jnp.broadcast_to(cond_act, (16, D))

    def weight(s, h, a, b):
        return w_ref[s, h, :, a:b]

    def forward(s, x):
        for h in range(2):
            rows = dot_nn(cond_rows, weight(s, h, COLS, COLS + MODH))[0:1]
            mod_s[s, 0:1, h * MODH : (h + 1) * MODH] = rows + bm_ref[s, :, h * MODH : (h + 1) * MODH]
        shift1, scale1, gate1, shift2, scale2, gate2 = (
            mod_s[s, 0:1, i * D : (i + 1) * D] for i in range(6)
        )
        n1, inv1 = norm_rows(x)
        n1_s[s] = n1
        inv1_s[s] = inv1
        normed = (n1 * (1.0 + scale1) + shift1).astype(BF)
        normed_s[s] = normed
        attended = jnp.broadcast_to(bo_ref[s], x.shape)
        for h in range(2):
            qkv = (dot_nn(normed, weight(s, h, 0, QKV)) + bqkv_ref[s, h]).astype(BF)
            qkv_s[s, h] = qkv
            mixed = []
            for i in range(3):
                q, k, v = (qkv[:, j * EH + i * HD : j * EH + (i + 1) * HD] for j in range(3))
                scores = dot_nt(q, k) * SCALING
                expo = jnp.exp(scores - jnp.max(scores, axis=-1, keepdims=True))
                probs = expo / jnp.sum(expo, axis=-1, keepdims=True)
                probs_s[s, 3 * h + i] = probs
                mixed.append(dot_nn(probs.astype(BF), v))
            mixed = jnp.concatenate(mixed, axis=1).astype(BF)
            mixed_s[s, h] = mixed
            attended = attended + dot_nt(mixed, weight(s, h, QKV, QKV + EH))
        attended_s[s] = attended
        hidden = x + gate1 * attended
        n2, inv2 = norm_rows(hidden)
        n2_s[s] = n2
        inv2_s[s] = inv2
        normed_two = (n2 * (1.0 + scale2) + shift2).astype(BF)
        normed_two_s[s] = normed_two
        down = jnp.broadcast_to(bd_ref[s], x.shape)
        at = QKV + EH
        for h in range(2):
            up = dot_nn(normed_two, weight(s, h, at, at + FH)) + bu_ref[s, h]
            c = math.sqrt(2.0 / math.pi)
            square = up * up
            tanh = jnp.tanh(c * (up + 0.044715 * (square * up)))
            half = 0.5 * (1.0 + tanh)
            activated = (up * half).astype(BF)
            activated_s[s, h] = activated
            slope_s[s, h] = half + (0.5 * c) * up * (1.0 - tanh * tanh) * (
                1.0 + (3 * 0.044715) * square
            )
            down = down + dot_nt(activated, weight(s, h, at + FH, at + 2 * FH))
        down_s[s] = down
        return hidden + gate2 * down

    def add_weight(h, a, b, value):
        if latents == 1:
            dw_out[h, :, a:b] = value.astype(BF)
        else:
            dw_s[h, :, a:b] += value

    def backward(s, g):
        shift1, scale1, gate1, shift2, scale2, gate2 = (
            mod_s[s, 0:1, i * D : (i + 1) * D] for i in range(6)
        )
        at = QKV + EH
        down_grad = (gate2 * g).astype(BF)
        n2_grad = None
        for h in range(2):
            active_grad = dot_nn(down_grad, weight(s, h, at + FH, at + 2 * FH))
            up_grad = (active_grad * slope_s[s, h]).astype(BF)
            upg_s[h] = up_grad
            part = dot_nt(up_grad, weight(s, h, at, at + FH))
            n2_grad = part if n2_grad is None else n2_grad + part
        n2 = n2_s[s]
        hidden_grad = g + norm_back(n2_grad * (1.0 + scale2), n2, inv2_s[s])
        attend_grad = (gate1 * hidden_grad).astype(BF)
        n1_grad = None
        for h in range(2):
            mixed_grad = dot_nn(attend_grad, weight(s, h, QKV, QKV + EH)).astype(BF)
            qkv = qkv_s[s, h]
            parts = [[], [], []]
            for i in range(3):
                q, k, v = (qkv[:, j * EH + i * HD : j * EH + (i + 1) * HD] for j in range(3))
                mg = mixed_grad[:, i * HD : (i + 1) * HD]
                probs = probs_s[s, 3 * h + i]
                parts[2].append(dot_tn(probs.astype(BF), mg))
                weighted = probs * dot_nt(mg, v)
                score_grad = (
                    weighted - probs * jnp.sum(weighted, axis=-1, keepdims=True)
                ).astype(BF)
                parts[0].append(dot_nn(score_grad, k) * SCALING)
                parts[1].append(dot_tn(score_grad, q) * SCALING)
            proj_grad = jnp.concatenate(parts[0] + parts[1] + parts[2], axis=1).astype(BF)
            pjg_s[h] = proj_grad
            part = dot_nt(proj_grad, weight(s, h, 0, QKV))
            n1_grad = part if n1_grad is None else n1_grad + part
        n1 = n1_s[s]
        input_grad = hidden_grad + norm_back(n1_grad * (1.0 + scale1), n1, inv1_s[s])
        back_s[...] = input_grad

        @pl.when(section == s)
        def _():
            grad_out[0] = input_grad
            mod_grad = jnp.concatenate(
                [
                    token_sum(n1_grad),
                    token_sum(n1_grad * n1),
                    token_sum(hidden_grad * attended_s[s]),
                    token_sum(n2_grad),
                    token_sum(n2_grad * n2),
                    token_sum(g * down_s[s]),
                ],
                axis=1,
            ).astype(BF)
            mod_rows = jnp.broadcast_to(mod_grad, (16, 6 * D))
            silu_grad = sum(
                dot_nt(
                    mod_rows[:, h * MODH : (h + 1) * MODH], weight(s, h, COLS, COLS + MODH)
                )[0:1]
                for h in range(2)
            )
            cond_grad = silu_grad * (sig * (1.0 + cond * (1.0 - sig)))
            pieces = [mod_grad.astype(F32)]
            pieces += [token_sum(pjg_s[h].astype(F32)) for h in range(2)]
            pieces += [token_sum(attend_grad.astype(F32))]
            pieces += [token_sum(upg_s[h].astype(F32)) for h in range(2)]
            pieces += [token_sum(down_grad.astype(F32)), cond_grad, cond_act.astype(F32)]
            small_out[0] = jnp.concatenate(pieces, axis=1)
            for h in range(2):
                add_weight(h, 0, QKV, dot_tn(normed_s[s], pjg_s[h]))
                add_weight(h, QKV, at, dot_tn(attend_grad, mixed_s[s, h]))
                add_weight(h, at, at + FH, dot_tn(normed_two_s[s], upg_s[h]))
                add_weight(h, at + FH, at + 2 * FH, dot_tn(down_grad, activated_s[s, h]))

    if latents > 1:

        @pl.when(pl.program_id(0) == 0)
        def _():
            dw_s[...] = jnp.zeros_like(dw_s)

    y0 = forward(0, x_ref[0].astype(F32)).astype(BF)

    @pl.when(section == 0)
    def _():
        act_out[0] = y0

    y1 = forward(1, y0.astype(F32))

    @pl.when(section == 1)
    def _():
        act_out[0] = y1.astype(BF)

    backward(1, g_ref[0])

    @pl.when(section == 0)
    def _():
        backward(0, back_s[...].astype(BF).astype(F32))

    if latents > 1:

        @pl.when(pl.program_id(0) == latents - 1)
        def _():
            dw_out[...] = dw_s[...].astype(BF)


def run_blocks(place, x, cond, g, w, bm, bqkv, bo, bu, bd, latents):
    length = x.shape[1]

    def picked(shape):
        return pl.BlockSpec(
            (1,) + shape, lambda i, place: (place[1] * latents + i,) + (0,) * len(shape)
        )

    def own(shape):
        return pl.BlockSpec((1,) + shape, lambda i, place: (i,) + (0,) * len(shape))

    def whole(a):
        return pl.BlockSpec(
            a.shape, lambda i, place: (0,) * a.ndim, pipeline_mode=pl.Buffered(1)
        )

    def kept(shape, dtype):
        return pltpu.VMEM(shape, dtype)

    def kernel(*refs):
        block_kernel(latents, *refs)

    t = length
    return pl.pallas_call(
        kernel,
        grid_spec=pltpu.PrefetchScalarGridSpec(
            num_scalar_prefetch=1,
            grid=(latents,),
            in_specs=[picked((t, D)), picked((1, D)), picked((t, D))]
            + [whole(a) for a in (w, bm, bqkv, bo, bu, bd)],
            out_specs=[
                own((t, D)),
                own((t, D)),
                pl.BlockSpec((2, D, COLS), lambda i, place: (0, 0, 0)),
                own((1, SMALL)),
            ],
            scratch_shapes=[
                kept((2, t, D), F32),
                kept((2, t, 1), F32),
                kept((2, t, D), BF),
                kept((2, 2, t, QKV), BF),
                kept((2, 6, t, t), F32),
                kept((2, 2, t, EH), BF),
                kept((2, t, D), F32),
                kept((2, t, D), F32),
                kept((2, t, 1), F32),
                kept((2, t, D), BF),
                kept((2, 2, t, FH), F32),
                kept((2, 2, t, FH), BF),
                kept((2, t, D), F32),
                kept((2, 8, 6 * D), F32),
                kept((2, t, FH), BF),
                kept((2, t, QKV), BF),
                kept((t, D), F32),
                kept((2, D, COLS) if latents > 1 else (8, 128), F32),
            ],
        ),
        out_shape=(
            jax.ShapeDtypeStruct((latents, t, D), BF),
            jax.ShapeDtypeStruct((latents, t, D), F32),
            jax.ShapeDtypeStruct((2, D, COLS), BF),
            jax.ShapeDtypeStruct((latents, 1, SMALL), F32),
        ),
        compiler_params=pltpu.CompilerParams(vmem_limit_bytes=58 * 1024 * 1024),
        cost_estimate=pl.CostEstimate(
            flops=12_000_000_000, bytes_accessed=16_000_000, transcendentals=2_000_000
        ),
    )(place, x, cond, g, w, bm, bqkv, bo, bu, bd)


def swapped(value, axis):
    return lax.ppermute(value, axis, [(0, 1), (1, 0)])


def both_halves(mine, other, half):
    first = jnp.where(half == 0, mine, other)
    second = jnp.where(half == 0, other, mine)
    return jnp.concatenate([first, second], axis=0)


def per_device(
    inputs,
    conditioning,
    out_grad,
    weight_mod,
    bias_mod,
    weight_qkv,
    bias_qv,
    weight_out,
    bias_out,
    first_feed_weight,
    first_feed_bias,
    second_feed_weight,
    second_feed_bias,
):
    section = lax.axis_index("pipe")
    half = lax.axis_index("heads")
    shard = lax.axis_index("shard")
    shards = lax.axis_size("shard")
    rows = weight_qkv.shape[1]
    latents = inputs.shape[0] // 2

    own_mod = lax.dynamic_slice_in_dim(weight_mod[0].reshape(rows, 2 * MODH), half * MODH, MODH, 1)
    own_bias = jnp.concatenate(
        [
            bias_mod.reshape(-1),
            bias_qv.reshape(-1),
            bias_out.reshape(-1),
            first_feed_bias.reshape(-1),
            second_feed_bias.reshape(-1),
        ]
    ).reshape(rows, BIAS_COLS)
    packed = jnp.concatenate(
        [
            weight_qkv.reshape(rows, QKV),
            weight_out[0].T,
            first_feed_weight[0],
            second_feed_weight[0].T,
            own_mod,
            own_bias,
            jnp.zeros((rows, PAD - BIAS_COLS), BF),
        ],
        axis=1,
    )
    gathered = gather_weights(packed)
    w = gathered.reshape(2, 2, shards * rows, WIDE)
    bias = (
        w[:, :, :, COLS + MODH : COLS + MODH + BIAS_COLS]
        .astype(F32)
        .reshape(2, 2, shards, rows * BIAS_COLS)
    )
    own_qv, own_up = EH // shards, FH // shards
    cut = [6 * rows, 2 * own_qv, rows, own_up, rows]
    ends = [sum(cut[: i + 1]) for i in range(5)]
    bm, bqv, bo, bu, bd = jnp.split(bias, ends[:-1], axis=-1)
    bm = bm[:, 0].reshape(2, shards, 6, rows).swapaxes(1, 2).reshape(2, 1, 6 * D)
    bqv = bqv.reshape(2, 2, shards, 2, own_qv).swapaxes(2, 3).reshape(2, 2, 2, EH)
    bqkv = jnp.concatenate([bqv[:, :, :1], jnp.zeros_like(bqv[:, :, :1]), bqv[:, :, 1:]], axis=2)
    bqkv = bqkv.reshape(2, 2, 1, QKV)
    bo = bo[:, 0].reshape(2, 1, D)
    bu = bu.reshape(2, 2, 1, FH)
    bd = bd[:, 0].reshape(2, 1, D)

    place = jnp.stack([section, half]).astype(jnp.int32)
    act, grad, dw, small = run_blocks(
        place,
        inputs,
        conditioning.astype(F32)[:, None, :],
        out_grad,
        w,
        bm,
        bqkv,
        bo,
        bu,
        bd,
        latents,
    )
    activations = both_halves(act, swapped(act, "heads"), half)[None]
    other_grad = swapped(grad.astype(BF), "heads").astype(F32)
    input_grads = both_halves(grad, other_grad, half)[None]

    small = jnp.broadcast_to(small.reshape(1, latents * SMALL), (4 * shards, latents * SMALL))
    small = lax.all_to_all(small, ("pipe", "heads", "shard"), 0, 0, tiled=True)
    small = small.reshape(2, 2, shards, latents, SMALL)
    cond_at = SMALL - 2 * D
    cond_grad = lax.dynamic_index_in_dim(small, shard, 2, keepdims=False)
    cond_grad = cond_grad[..., cond_at : cond_at + D].sum(axis=0).reshape(2 * latents, D)
    mine = lax.dynamic_index_in_dim(small, section, 0, keepdims=False).reshape(-1, SMALL)
    mod_grad = mine[:, : 6 * D].astype(BF)
    cond_act = lax.dynamic_slice_in_dim(mine[:, SMALL - D :], shard * rows, rows, 1).astype(BF)
    grad_mod = dot_tn(cond_act, mod_grad).reshape(1, rows, 6, D)
    sums = mine[:, : cond_at].sum(axis=0)
    grad_bias_mod = lax.dynamic_slice_in_dim(sums[: 6 * D].reshape(6, D), shard * rows, rows, 1)
    at = 6 * D
    proj = sums[at : at + 2 * QKV].reshape(2, 3, EH)
    proj = lax.dynamic_index_in_dim(proj, half, 0, keepdims=False)
    proj = lax.dynamic_slice_in_dim(proj, shard * own_qv, own_qv, 1)
    grad_bias_qv = jnp.stack([proj[0], proj[2]])
    at += 2 * QKV
    grad_bias_out = lax.dynamic_slice_in_dim(sums, at + shard * rows, rows)
    at += D
    grad_bias_up = lax.dynamic_slice_in_dim(sums, at + half * FH + shard * own_up, own_up)
    at += 2 * FH
    grad_bias_down = lax.dynamic_slice_in_dim(sums, at + shard * rows, rows)

    total = reduce_weights(dw.reshape(2, shards, rows, COLS))
    at = QKV + EH
    return (
        activations,
        input_grads,
        cond_grad,
        grad_mod,
        grad_bias_mod[None],
        total[:, :QKV].reshape(1, rows, 3, EH),
        grad_bias_qv[None],
        total[:, QKV:at].T[None],
        grad_bias_out[None],
        total[:, at : at + FH][None],
        grad_bias_up[None],
        total[:, at + FH :].T[None],
        grad_bias_down[None],
    )


def gather_weights(packed):
    return lax.all_gather(packed, ("pipe", "heads", "shard"))


def reduce_weights(dw):
    tiles = dw.reshape(-1, *dw.shape[2:])
    arrived = lax.all_to_all(tiles, ("heads", "shard"), 0, 0, tiled=True)
    return arrived.astype(F32).sum(axis=0)


def solution(mesh):
    return jax.shard_map(
        per_device,
        mesh=mesh,
        in_specs=(
            P("shard", None, None),
            P("shard", None),
            P("shard", None, None),
            P("pipe", "shard", None, None),
            P("pipe", None, "shard"),
            P("pipe", "shard", None, "heads"),
            P("pipe", None, ("heads", "shard")),
            P("pipe", "heads", "shard"),
            P("pipe", "shard"),
            P("pipe", "shard", "heads"),
            P("pipe", ("heads", "shard")),
            P("pipe", "heads", "shard"),
            P("pipe", "shard"),
        ),
        out_specs=(
            P("pipe", "shard", None, None),
            P("pipe", "shard", None, None),
            P("shard", None),
            P("pipe", "shard", None, None),
            P("pipe", None, "shard"),
            P("pipe", "shard", None, "heads"),
            P("pipe", None, ("heads", "shard")),
            P("pipe", "heads", "shard"),
            P("pipe", "shard"),
            P("pipe", "shard", "heads"),
            P("pipe", ("heads", "shard")),
            P("pipe", "heads", "shard"),
            P("pipe", "shard"),
        ),
        check_vma=False,
    )
```

time: 859 us -> 258 us (0.30); the launches traced: 846 us -> 255 us
  blocking collectives: 286 us -> 26 us
  starting transfers between devices: 115 us -> 5.95 us
  other arithmetic: 116 us -> 9.11 us
  local copies, waits for them, and re-layouts: 104 us -> 29.6 us
  matrix products: 69.5 us -> 2 us
  Pallas kernels: 0 us -> 26.1 us
    all_gather x18 -> x0, blocking collectives: 259 us -> none  [the longest x12 67.9 us: head_total(): lax.all_gather(share.astype(jnp.bfloat16), 'heads', axis=1, tiled=True)]
    all_to_all x23 -> x1, starting transfers between devices: 109 us -> 3.75 us  [reduce_weights(): arrived = lax.all_to_all(tiles, ('heads', 'shard'), 0, 0, tiled=True)]
    all_gather x1, waiting for transfers between devices: 0.02 us -> 90.1 us  [gather_weights(): return lax.all_gather(packed, ('pipe', 'heads', 'shard'))]
    all_to_all x23 -> x1, waiting for transfers between devices: 90.3 us -> 17.5 us  [reduce_weights(): arrived = lax.all_to_all(tiles, ('heads', 'shard'), 0, 0, tiled=True)]
    reduce_sum x58 -> x3, other arithmetic: 67.2 us -> 1.16 us  [the longest x1 0.58 us: per_device(): cond_grad[..., cond_at:cond_at + D].sum(axis=0).reshape(2 * latents, D)]
    dot_general x54 -> x1, matrix products: 63.9 us -> 2 us  [dot_tn(): lax.dot_general(a, b, (((0,), (0,)), ((), ())), preferred_element_type=F32)]
    reduce_scatter x12 -> x0, waiting for transfers between devices: 44.6 us -> none  [head_total(): lax.psum_scatter(partial_sum.astype(jnp.bfloat16), 'heads', scatter_dimen...]
    another operation x54 -> x3, local copies, waits for them, and re-layouts: 41.6 us -> 1.39 us  [the longest x1 0.66 us: per_device(): bo = bo[:, 0].reshape(2, 1, D)]
  transfers between devices with their start and end apart: 40 -> 4, of which waited for: 23 -> 4; matrix products, arithmetic and copies ran while one was open for 26% -> 9% of each run, Pallas kernels for 0% -> 0%
where the time goes in v1:
time: 258 us; the launch traced here: 255 us
  waiting for transfers between devices  142 us (55%)
  local copies, waits for them, and re-layouts  29.6 us (11%)
  Pallas kernels  26.1 us (10%)
  blocking collectives  26 us (10%)
  between operations  14.2 us (6%)
  other arithmetic  9.11 us (4%)
  starting transfers between devices  5.95 us (2%)
    all_gather x1, waiting for transfers between devices, gather_weights(): return lax.all_gather(packed, ('pipe', 'heads', 'shard'))  90.1 us
    ppermute x2, waiting for transfers between devices, swapped(): return lax.ppermute(value, axis, [(0, 1), (1, 0)])  34.8 us
    pallas_call x1, Pallas kernels, run_blocks(): pl.pallas_call(kernel, grid_spec=pltpu.PrefetchScalarGridSpec(num_scalar_...  26.1 us
    all_to_all x1, blocking collectives, per_device(): small = lax.all_to_all(small, ('pipe', 'heads', 'shard'), 0, 0, tiled=True)  26 us
    all_to_all x1, waiting for transfers between devices, reduce_weights(): arrived = lax.all_to_all(tiles, ('heads', 'shard'), 0, 0, tiled=True)  17.5 us
  transfers between devices with their start and end apart: 4, of which 4 were waited for; matrix products, arithmetic and copies ran while one was open for 9% of the time, Pallas kernels for 0%

profile of v1, /device:TPU:0, one launch (start us, length us, event | category | flops | bytes accessed | tf_op | source)
XLA Modules:
  0.0 255.3 jit_solution(9957895470597195718)
XLA Ops:
  7.2 1.0 copy.53
  8.2 0.9 copy.44
  10.8 2.1 concatenate.15
  13.0 1.8 concatenate.16
  14.8 1.3 reshape.139.refs_2_
  16.7 90.1 %all-gather.3.cloned.1.call-done = bf16[1536,3584]{1,0:T(8,128)(2,1)} async-done(((bf16[48,3584]{1,0:T(8,128)(2,1)}), bf16[1536,3584]{1,0:T(8,128)(2,1)}) %all-gather.3.cloned.1.call-update) | async-done | bytes 11010064 | tf_op jit(solution)/shard_map/all_gather | solution.py:467
  106.8 1.0 slice_convert_fusion
  112.2 26.1 %shard_map.228 = (bf16[1,256,384]{2,1,0:T(8,128)(2,1)}, f32[1,256,384]{2,1,0:T(8,128)}, bf16[2,384,2304]{2,1,0:T(8,128)(2,1)}, f32[1,1,6528]{2,1,0:T(1,128)}) custom-call(s32[2]{0:T(128)} %pad_add_fusion.refs_0_, bf16[2,256,384]{2,1,0:T(8,128)(2,1)} %refs_1_.1, f32[2,1,384]{2,1,0:T(1,128)} %reshape.139.refs_2_, f32[2,256,384]{2,1,0:T(8,128)} %refs_3_.1, ...), custom_call_target="tpu_custom_call" | custom-call | flops 12000000000 | bytes 16000000 | tf_op jit(solution)/shard_map/pallas_call | solution.py:285
  139.5 26.0 %all_to_all.11 = f32[32,1,6528]{2,1,0:T(1,128)} all-to-all(f32[32,1,6528]{2,1,0:T(1,128)S(1)} %broadcast_in_dim.52), channel_id=1, replica_groups=mesh['pipe'=2,'heads'=2,'shard'=8] {'pipe','heads','shard'}, dimensions={0} | all-to-all | bytes 1671168 | tf_op jit(solution)/shard_map/all_to_all | solution.py:424
  165.4 3.8 %all-to-all-start.1 = ((bf16[16,48,2304]{2,1,0:T(8,128)(2,1)}), bf16[16,48,2304]{2,1,0:T(8,128)(2,1)S(1)}, u32[]{:S(2)}, u32[]{:S(2)}) async-start(bf16[16,48,2304]{2,1,0:T(8,128)(2,1)} %bitcast.70), calls=%async_computation.1 | async-start | bytes 7077888 | tf_op jit(solution)/shard_map/all_to_all | solution.py:472
  169.2 1.9 collective-permute-start
  171.0 1.0 convert_element_type.15
  172.4 33.1 %collective-permute-done = bf16[1,256,384]{2,1,0:T(8,128)(2,1)} collective-permute-done((bf16[1,256,384]{2,1,0:T(8,128)(2,1)}, bf16[1,256,384]{2,1,0:T(8,128)(2,1)}, u32[]{:S(2)}, u32[]{:S(2)}) %collective-permute-start) | collective-permute-done | bytes 196640 | tf_op jit(solution)/shard_map/ppermute | solution.py:333
  205.5 1.1 broadcast_select_fusion.1
  207.4 1.6 collective-permute-done.1
  209.0 1.1 convert_select_fusion.1
  211.0 1.0 constant_dynamic-slice_fusion.2
  213.5 1.4 reshape.138
  214.9 2.0 fusion
  216.9 1.9 reshape.136
  218.8 1.9 copy.49
  223.6 1.3 dynamic-slice_bitcast_fusion.1
  226.3 1.3 dynamic-slice_bitcast_fusion
  228.2 17.5 %all-to-all-done.1 = bf16[16,48,2304]{2,1,0:T(8,128)(2,1)S(1)} async-done(((bf16[16,48,2304]{2,1,0:T(8,128)(2,1)}), bf16[16,48,2304]{2,1,0:T(8,128)(2,1)S(1)}, u32[]{:S(2)}, u32[]{:S(2)}) %all-to-all-start.1) | async-done | bytes 3538976 | tf_op jit(solution)/shard_map/all_to_all | solution.py:472
  (56 shorter events, 19.1 us)
Async XLA Ops:
  7.2 99.7 %all-gather.3.cloned.1.call-start = ((), (), s32[]{:S(2)}) async-start(), calls=%async_computation.2 | async-start | bytes 11354112 | tf_op jit(solution)/shard_map/all_gather | solution.py:467
  165.4 80.3 %all-to-all-start.1 = ((bf16[16,48,2304]{2,1,0:T(8,128)(2,1)}), bf16[16,48,2304]{2,1,0:T(8,128)(2,1)S(1)}, u32[]{:S(2)}, u32[]{:S(2)}) async-start(bf16[16,48,2304]{2,1,0:T(8,128)(2,1)} %bitcast.70), calls=%async_computation.1 | async-start | bytes 7077888 | tf_op jit(solution)/shard_map/all_to_all | solution.py:472
  169.2 36.3 %collective-permute-start = (bf16[1,256,384]{2,1,0:T(8,128)(2,1)}, bf16[1,256,384]{2,1,0:T(8,128)(2,1)}, u32[]{:S(2)}, u32[]{:S(2)}) collective-permute-start(bf16[1,256,384]{2,1,0:T(8,128)(2,1)} %get-tuple-element.17), channel_id=1, source_target_pairs={{0,8},{8,0},{1,9},{9,1},{2,10},{10,2},{3,11},{11,3},{4,12},{12,4},... | collective-permute-start | bytes 589832 | tf_op jit(solution)/shard_map/ppermute | solution.py:333
  172.1 36.9 %collective-permute-start.1 = (bf16[1,256,384]{2,1,0:T(8,128)(2,1)S(1)}, bf16[1,256,384]{2,1,0:T(8,128)(2,1)S(1)}, u32[]{:S(2)}, u32[]{:S(2)}) collective-permute-start(bf16[1,256,384]{2,1,0:T(8,128)(2,1)S(1)} %convert_element_type.15), channel_id=1, source_target_pairs={{0,8},{8,0},{1,9},{9,1},{2,10},{10,2},{3,11},{11,3},{4,12},{12,4},... | collective-permute-start | bytes 589832 | tf_op jit(solution)/shard_map/ppermute | solution.py:333
  212.1 0.8 copy-start
  212.9 0.6 copy-start.1
Sparse Core Ops, SparseCore 0:
  14.9 91.8 all-gather.2

commit v2 on v1

--- a/solution.py
+++ b/solution.py
@@ -416,19 +416,25 @@
         bd,
         latents,
     )
-    activations = both_halves(act, swapped(act, "heads"), half)[None]
-    other_grad = swapped(grad.astype(BF), "heads").astype(F32)
-    input_grads = both_halves(grad, other_grad, half)[None]
-
-    small = jnp.broadcast_to(small.reshape(1, latents * SMALL), (4 * shards, latents * SMALL))
-    small = lax.all_to_all(small, ("pipe", "heads", "shard"), 0, 0, tiled=True)
-    small = small.reshape(2, 2, shards, latents, SMALL)
+    padded = -(-SMALL // 1024) * 1024
+    small = jnp.pad(small.reshape(latents, SMALL), ((0, 0), (0, padded - SMALL)))
+    total, small, sibling, act_other, grad_other = exchange(
+        dw.reshape(2, shards, rows, COLS),
+        small.reshape(latents, padded // 128, 128),
+        act,
+        grad.astype(BF),
+    )
+    activations = both_halves(act, act_other, half)[None]
+    input_grads = both_halves(grad, grad_other.astype(F32), half)[None]
+
+    small = small.reshape(2, shards, latents, padded)
+    sibling = sibling.reshape(2, latents, padded)
     cond_at = SMALL - 2 * D
-    cond_grad = lax.dynamic_index_in_dim(small, shard, 2, keepdims=False)
-    cond_grad = cond_grad[..., cond_at : cond_at + D].sum(axis=0).reshape(2 * latents, D)
-    mine = lax.dynamic_index_in_dim(small, section, 0, keepdims=False).reshape(-1, SMALL)
+    cond_grad = lax.dynamic_index_in_dim(small, shard, 1, keepdims=False) + sibling
+    cond_grad = cond_grad[..., cond_at : cond_at + D].reshape(2 * latents, D)
+    mine = small.reshape(-1, padded)
     mod_grad = mine[:, : 6 * D].astype(BF)
-    cond_act = lax.dynamic_slice_in_dim(mine[:, SMALL - D :], shard * rows, rows, 1).astype(BF)
+    cond_act = lax.dynamic_slice_in_dim(mine[:, SMALL - D : SMALL], shard * rows, rows, 1).astype(BF)
     grad_mod = dot_tn(cond_act, mod_grad).reshape(1, rows, 6, D)
     sums = mine[:, : cond_at].sum(axis=0)
     grad_bias_mod = lax.dynamic_slice_in_dim(sums[: 6 * D].reshape(6, D), shard * rows, rows, 1)
@@ -444,7 +450,6 @@
     at += 2 * FH
     grad_bias_down = lax.dynamic_slice_in_dim(sums, at + shard * rows, rows)
 
-    total = reduce_weights(dw.reshape(2, shards, rows, COLS))
     at = QKV + EH
     return (
         activations,
@@ -463,14 +468,238 @@
     )
 
 
+def ring_place():
+    shards = lax.axis_size("shard")
+    shard = lax.axis_index("shard")
+    return jnp.where(shard % 2 == 0, shard // 2, shards - 1 - shard // 2)
+
+
+def ring_shard(position):
+    shards = lax.axis_size("shard")
+    position = lax.rem(position + 2 * shards, shards)
+    return jnp.where(position < shards // 2, 2 * position, 2 * (shards - 1 - position) + 1)
+
+
+def greet(devices):
+    barrier = pltpu.get_barrier_semaphore()
+    for device in devices:
+        pl.semaphore_signal(
+            barrier, inc=1, device_id=device, device_id_type=pl.DeviceIdType.MESH
+        )
+    pl.semaphore_wait(barrier, len(devices))
+
+
+def neighbours():
+    r = ring_place()
+    return (
+        {"shard": ring_shard(r + 1)},
+        {"shard": ring_shard(r - 1)},
+        {"heads": 1 - lax.axis_index("heads")},
+        {"pipe": 1 - lax.axis_index("pipe")},
+    )
+
+
+def remote(src, dst, send, recv, device):
+    copy = pltpu.make_async_remote_copy(
+        src_ref=src,
+        dst_ref=dst,
+        send_sem=send,
+        recv_sem=recv,
+        device_id=device,
+        device_id_type=pl.DeviceIdType.MESH,
+    )
+    return copy
+
+
+def gather_kernel(shards, split, packed, out, own_sem, send, recv):
+    p, h = lax.axis_index("pipe"), lax.axis_index("heads")
+    r = ring_place()
+    after, before, across, core = neighbours()
+    forward_hops, back_hops = shards // 2, shards // 2 - 1
+    greet([after, before, across, core])
+
+    def chunk(half, away):
+        return out.at[p, half, ring_shard(r - away)]
+
+    def part(half, away, a, b):
+        return out.at[p, half, ring_shard(r - away), :, a:b]
+
+    started = []
+
+    def go(ref, kind, sem_at, device):
+        copy = remote(ref, ref, send.at[kind, sem_at], recv.at[kind, sem_at], device)
+        copy.start()
+        started.append(copy)
+
+    def wait_for(ref, kind, sem_at):
+        remote(ref, ref, send.at[kind, sem_at], recv.at[kind, sem_at], core).wait_recv()
+
+    def along(half, away, a, b, kind):
+        if 0 <= away < forward_hops:
+            go(part(half, away, a, b), kind, (away + 1) % shards, after)
+        if -back_hops < away <= 0:
+            go(part(half, away, a, b), kind, (away - 1) % shards, before)
+
+    own = pltpu.make_async_copy(packed, chunk(h, 0), own_sem)
+    own.start()
+    own.wait()
+    order = [0]
+    for k in range(1, forward_hops + 1):
+        order += [k] + ([-k] if k <= back_hops else [])
+    for away in order:
+        if away != 0:
+            wait_for(chunk(h, away), 0, away % shards)
+        if away == 0:
+            go(part(h, 0, split, WIDE), 3, 0, across)
+        along(h, away, 0, WIDE, 0)
+        go(part(h, away, 0, split), 2, away % shards, across)
+        go(chunk(h, away), 4, away % shards, core)
+        if away == 0:
+            wait_for(part(1 - h, 0, split, WIDE), 3, 0)
+        else:
+            wait_for(part(1 - h, away, split, WIDE), 1, away % shards)
+        along(1 - h, away, split, WIDE, 1)
+    for away in order:
+        wait_for(part(1 - h, away, 0, split), 2, away % shards)
+        go(chunk(1 - h, away), 5, away % shards, core)
+    for away in order:
+        for kind, half in ((4, h), (5, 1 - h)):
+            ref = out.at[1 - p, half, ring_shard(r - away)]
+            wait_for(ref, kind, away % shards)
+    for copy in started:
+        copy.wait_send()
+
+
 def gather_weights(packed):
-    return lax.all_gather(packed, ("pipe", "heads", "shard"))
-
-
-def reduce_weights(dw):
-    tiles = dw.reshape(-1, *dw.shape[2:])
-    arrived = lax.all_to_all(tiles, ("heads", "shard"), 0, 0, tiled=True)
-    return arrived.astype(F32).sum(axis=0)
+    shards = lax.axis_size("shard")
+
+    def kernel(*refs):
+        gather_kernel(shards, 16 * 128, *refs)
+
+    return pl.pallas_call(
+        kernel,
+        in_specs=[pl.BlockSpec(memory_space=pl.ANY)],
+        out_specs=pl.BlockSpec(memory_space=pl.ANY),
+        out_shape=jax.ShapeDtypeStruct((2, 2, shards) + packed.shape, BF),
+        scratch_shapes=[
+            pltpu.SemaphoreType.DMA,
+            pltpu.SemaphoreType.DMA((6, shards)),
+            pltpu.SemaphoreType.DMA((6, shards)),
+        ],
+        compiler_params=pltpu.CompilerParams(collective_id=1, has_side_effects=True),
+    )(packed)
+
+
+def exchange_kernel(
+    shards, dw, small, act, grad, total, smalls, siblings, act_other, grad_other,
+    slots, moving, crossing, crossed, send, recv,
+):
+    h = lax.axis_index("heads")
+    r = ring_place()
+    after, before, across, core = neighbours()
+    forward_hops, back_hops = shards // 2, shards // 2 - 1
+    greet([after, before, across, core])
+    started = []
+
+    def go(src, dst, kind, at, device):
+        copy = remote(src, dst, send.at[kind, at], recv.at[kind, at], device)
+        copy.start()
+        started.append(copy)
+
+    def wait_for(ref, kind, at):
+        remote(ref, ref, send.at[kind, at], recv.at[kind, at], core).wait_recv()
+
+    def own_part(half, away):
+        return dw.at[half, ring_shard(r + away)]
+
+    ways = [(after, forward_hops, 1, 0), (before, back_hops, -1, forward_hops)]
+    for half in range(2):
+        for device, hops, sign, first in ways:
+            go(own_part(half, sign * hops), slots.at[first, half], half, first, device)
+    go(small, smalls.at[h, ring_shard(r)], 2, 1, after)
+    go(small, smalls.at[h, ring_shard(r)], 2, shards - 1, before)
+    go(small, smalls.at[h, ring_shard(r)], 3, 0, across)
+    go(act, act_other, 4, 0, across)
+    go(grad, grad_other, 4, 1, across)
+    smalls[h, ring_shard(r)] = small[...]
+    for hop in range(forward_hops):
+        for half in range(2):
+            for device, hops, sign, first in ways:
+                if hop < hops - 1:
+                    at = first + hop
+                    wait_for(slots.at[at, half], half, at)
+                    moving[at, half] = (
+                        slots[at, half].astype(F32)
+                        + own_part(half, sign * (hops - 1 - hop))[...].astype(F32)
+                    ).astype(BF)
+                    go(moving.at[at, half], slots.at[at + 1, half], half, at + 1, device)
+        for away, device in ((hop + 1, after), (-hop - 1, before)):
+            hops = forward_hops if away > 0 else back_hops
+            if abs(away) <= hops:
+                row = smalls.at[h, ring_shard(r - away)]
+                wait_for(row, 2, away % shards)
+                if abs(away) < hops:
+                    go(row, row, 2, (away + (1 if away > 0 else -1)) % shards, device)
+                go(row, row, 3, away % shards, across)
+    ends = [forward_hops - 1, shards - 2]
+    for half in range(2):
+        for at in ends:
+            wait_for(slots.at[at, half], half, at)
+
+    def summed(half):
+        value = dw[half, ring_shard(r)].astype(F32)
+        for at in ends:
+            value = value + slots[at, half].astype(F32)
+        return value
+
+    crossing[...] = summed(1 - h).astype(BF)
+    go(crossing, crossed, 4, 2, across)
+    for away in range(shards):
+        wait_for(smalls.at[1 - h, ring_shard(r - away)], 3, away)
+    for half in range(2):
+        go(smalls.at[half, ring_shard(r)], siblings.at[half], 5, half, core)
+    total[...] = summed(h)
+    wait_for(crossed, 4, 2)
+    total[...] += crossed[...].astype(F32)
+    wait_for(act_other, 4, 0)
+    wait_for(grad_other, 4, 1)
+    for half in range(2):
+        wait_for(siblings.at[half], 5, half)
+    for copy in started:
+        copy.wait_send()
+
+
+def exchange(dw, small, act, grad):
+    shards = dw.shape[1]
+    part = dw.shape[2:]
+
+    def kernel(*refs):
+        exchange_kernel(shards, *refs)
+
+    vmem = pl.BlockSpec(memory_space=pltpu.VMEM)
+    return pl.pallas_call(
+        kernel,
+        in_specs=[vmem] * 4,
+        out_specs=[vmem] * 5,
+        out_shape=(
+            jax.ShapeDtypeStruct(part, F32),
+            jax.ShapeDtypeStruct((2, shards) + small.shape, F32),
+            jax.ShapeDtypeStruct((2,) + small.shape, F32),
+            jax.ShapeDtypeStruct(act.shape, BF),
+            jax.ShapeDtypeStruct(grad.shape, BF),
+        ),
+        scratch_shapes=[
+            pltpu.VMEM((shards - 1, 2) + part, BF),
+            pltpu.VMEM((shards - 1, 2) + part, BF),
+            pltpu.VMEM(part, BF),
+            pltpu.VMEM(part, BF),
+            pltpu.SemaphoreType.DMA((6, shards)),
+            pltpu.SemaphoreType.DMA((6, shards)),
+        ],
+        compiler_params=pltpu.CompilerParams(
+            collective_id=2, has_side_effects=True, vmem_limit_bytes=50 * 1024 * 1024
+        ),
+    )(dw, small, act, grad)
 
 
 def solution(mesh):

time: 258 us -> 171 us (0.66)
  waiting for transfers between devices: 142 us -> 0 us
  Pallas kernels: 26.1 us -> 143 us
  blocking collectives: 26 us -> 0 us
  between operations: 14.2 us -> 0.85 us
  local copies, waits for them, and re-layouts: 29.6 us -> 19.5 us
  starting transfers between devices: 5.95 us -> 0 us
    pallas_call x0 -> x2, Pallas kernels: none -> 117 us  [the longest x1 65.3 us: gather_weights(): pl.pallas_call(kernel, in_specs=[pl.BlockSpec(memory_space=pl.ANY)], out_...]
    all_gather x1 -> x0, waiting for transfers between devices: 90.1 us -> none  [gather_weights(): return lax.all_gather(packed, ('pipe', 'heads', 'shard'))]
    ppermute x2 -> x0, waiting for transfers between devices: 34.8 us -> none  [swapped(): return lax.ppermute(value, axis, [(0, 1), (1, 0)])]
    all_to_all x1 -> x0, blocking collectives: 26 us -> none  [per_device(): small = lax.all_to_all(small, ('pipe', 'heads', 'shard'), 0, 0, tiled=True)]
    all_to_all x1 -> x0, waiting for transfers between devices: 17.5 us -> none  [reduce_weights(): arrived = lax.all_to_all(tiles, ('heads', 'shard'), 0, 0, tiled=True)]
    all_to_all x1 -> x0, starting transfers between devices: 3.75 us -> none  [reduce_weights(): arrived = lax.all_to_all(tiles, ('heads', 'shard'), 0, 0, tiled=True)]
  transfers between devices with their start and end apart: 4 -> 0, of which waited for: 4 -> 0; matrix products, arithmetic and copies ran while one was open for 9% -> 0% of each run, Pallas kernels for 0% -> 0%
where the time goes in v2:
time: 171 us
  Pallas kernels  143 us (84%)
  local copies, waits for them, and re-layouts  19.5 us (11%)
  other arithmetic  6.8 us (4%)
    pallas_call x1, Pallas kernels, gather_weights(): pl.pallas_call(kernel, in_specs=[pl.BlockSpec(memory_space=pl.ANY)], out_...  65.3 us
    pallas_call x1, Pallas kernels, exchange(): pl.pallas_call(kernel, in_specs=[vmem] * 4, out_specs=[vmem] * 5, out_sha...  51.9 us
    pallas_call x1, Pallas kernels, run_blocks(): pl.pallas_call(kernel, grid_spec=pltpu.PrefetchScalarGridSpec(num_scalar_...  26.3 us
    unnamed x12, local copies, waits for them, and re-layouts  4.48 us

profile of v2, /device:TPU:0, one launch (start us, length us, event | category | flops | bytes accessed | tf_op | source)
XLA Modules:
  0.0 170.9 jit_solution(5902910776482766350)
XLA Ops:
  0.7 1.0 copy.41
  1.6 0.9 copy.33
  2.7 0.8 reshape.139
  3.5 0.7 reshape.140
  4.2 2.1 %concatenate.15 = bf16[528]{0:T(1024)(128)(2,1)S(1)} concatenate(bf16[288]{0:T(512)(128)(2,1)S(1)} %reshape.139, bf16[48]{0:T(256)(128)(2,1)S(1)} %reshape.140, bf16[48]{0:T(256)(128)(2,1)} %bitcast.96, bf16[96]{0:T(256)(128)(2,1)} %bitcast.97, bf16[48]{0:T(256)(128)(2,1)} %bitcast.98), dimensions={0} | concatenate | bytes 2112 | tf_op jit(solution)/shard_map/concatenate | solution.py:365
  6.4 1.8 %concatenate.16.refs_0_ = bf16[48,3584]{1,0:T(8,128)(2,1)} concatenate(bf16[48,576]{1,0:T(8,128)(2,1)S(1)} %reshape.138, bf16[48,192]{1,0:T(8,128)(2,1)} %bitcast.95, bf16[48,768]{1,0:T(8,128)(2,1)} %bitcast.91, bf16[48,768]{1,0:T(8,128)(2,1)} %bitcast.92, bf16[48,1152]{1,0:T(8,128)(2,1)S(1)} %constant_dynamic-slice_fusion.3, bf16[48,11]{1,0:T(8,128)(2,1)S(1)} %reshape.144, ...), dimensions={1} | concatenate | bytes 688128 | tf_op jit(solution)/shard_map/concatenate | solution.py:374
  8.2 65.3 %shard_map.228 = bf16[2,2,8,48,3584]{4,3,2,1,0:T(8,128)(2,1)} custom-call(bf16[48,3584]{1,0:T(8,128)(2,1)} %concatenate.16.refs_0_), custom_call_target="tpu_custom_call" | custom-call | tf_op jit(solution)/shard_map/pallas_call | solution.py:579
  73.5 1.0 slice_convert_fusion
  75.3 0.7 reshape.165.refs_6_
  76.1 0.7 reshape_squeeze.14.refs_7_
  77.5 0.7 reshape.148.refs_5_
  78.3 0.7 reshape.152.refs_8_
  80.1 26.3 %shard_map.229 = (bf16[1,256,384]{2,1,0:T(8,128)(2,1)}, f32[1,256,384]{2,1,0:T(8,128)}, bf16[2,384,2304]{2,1,0:T(8,128)(2,1)}, f32[1,1,6528]{2,1,0:T(1,128)}) custom-call(s32[2]{0:T(128)} %pad_add_fusion.refs_0_, bf16[2,256,384]{2,1,0:T(8,128)(2,1)} %refs_1_.1, f32[2,1,384]{2,1,0:T(1,128)} %reshape.162.refs_2_, f32[2,256,384]{2,1,0:T(8,128)} %refs_3_.1, ...), custom_call_target="tpu_custom_call" | custom-call | flops 12000000000 | bytes 16000000 | tf_op jit(solution)/shard_map/pallas_call | solution.py:285
  106.4 1.1 convert_element_type.14.refs_3_
  107.5 0.8 pad.4
  108.2 0.9 copy-done
  109.1 51.9 %shard_map.230 = (f32[48,2304]{1,0:T(8,128)S(1)}, f32[2,8,1,56,128]{4,3,2,1,0:T(8,128)S(1)}, f32[2,1,56,128]{3,2,1,0:T(8,128)S(1)}, bf16[1,256,384]{2,1,0:T(8,128)(2,1)S(1)}, bf16[1,256,384]{2,1,0:T(8,128)(2,1)S(1)}) custom-call(bf16[2,8,48,2304]{3,2,1,0:T(8,128)(2,1)} %bitcast.83, f32[1,56,128]{2,1,0:T(8,128)S(1)} %bitcast.80, ...), custom_call_target="tpu_custom_call" | custom-call | tf_op jit(solution)/shard_map/pallas_call | solution.py:680
  162.4 0.8 copy.38
  164.0 1.0 convert_select_fusion.1
  165.0 0.9 maximum_bitcast_fusion
  166.0 0.8 maximum_bitcast_fusion.1
  168.8 0.7 copy.39
  169.5 0.7 slice_bitcast_fusion
  170.2 0.7 slice_bitcast_fusion.2
  (49 shorter events, 7.1 us)
Async XLA Ops:
  0.6 78.9 %copy-start.2 = (bf16[2,384]{1,0:T(2,128)(2,1)S(1)}, bf16[2,384]{1,0:T(2,128)(2,1)}, u32[]{:S(2)}) copy-start(bf16[2,384]{1,0:T(2,128)(2,1)} %param.14) | copy-start | bytes 4612
  106.4 59.6 %copy-start.1 = (bf16[1,256,384]{2,1,0:T(8,128)(2,1)S(1)}, bf16[1,256,384]{2,1,0:T(8,128)(2,1)}, u32[]{:S(2)}) copy-start(bf16[1,256,384]{2,1,0:T(8,128)(2,1)} %get-tuple-element.22.refs_2_) | copy-start | bytes 589828
  108.2 0.9 copy-start

commit v3 on v2

--- a/solution.py
+++ b/solution.py
@@ -526,38 +526,51 @@
 
     started = []
 
-    def go(ref, kind, sem_at, device):
-        copy = remote(ref, ref, send.at[kind, sem_at], recv.at[kind, sem_at], device)
+    def go(ref, kind, sem_at, device, src=None):
+        src = ref if src is None else src
+        copy = remote(src, ref, send.at[kind, sem_at], recv.at[kind, sem_at], device)
         copy.start()
         started.append(copy)
 
     def wait_for(ref, kind, sem_at):
         remote(ref, ref, send.at[kind, sem_at], recv.at[kind, sem_at], core).wait_recv()
 
-    def along(half, away, a, b, kind):
-        if 0 <= away < forward_hops:
-            go(part(half, away, a, b), kind, (away + 1) % shards, after)
+    def along(half, away, a, b, kind, src=None):
+        mid = (a + b) // 2
+        if 0 <= away < forward_hops - 1:
+            go(part(half, away, a, b), kind, away + 1, after, src)
+        elif away == forward_hops - 1:
+            go(part(half, away, a, mid), kind, forward_hops, after)
         if -back_hops < away <= 0:
-            go(part(half, away, a, b), kind, (away - 1) % shards, before)
-
-    own = pltpu.make_async_copy(packed, chunk(h, 0), own_sem)
-    own.start()
-    own.wait()
+            go(part(half, away, a, b), kind, (away - 1) % shards, before, src)
+        elif away == -back_hops:
+            go(part(half, away, mid, b), kind, 0, before)
+
+    def arrived(half, away, a, b, kind):
+        mid = (a + b) // 2
+        if away == forward_hops:
+            wait_for(part(half, away, a, mid), kind, forward_hops)
+            wait_for(part(half, away, mid, b), kind, 0)
+        else:
+            wait_for(part(half, away, a, b), kind, away % shards)
+
     order = [0]
     for k in range(1, forward_hops + 1):
         order += [k] + ([-k] if k <= back_hops else [])
-    for away in order:
-        if away != 0:
-            wait_for(chunk(h, away), 0, away % shards)
-        if away == 0:
-            go(part(h, 0, split, WIDE), 3, 0, across)
+    own = pltpu.make_async_copy(packed, chunk(h, 0), own_sem)
+    own.start()
+    go(part(h, 0, split, WIDE), 3, 0, across, packed.at[:, split:WIDE])
+    along(h, 0, 0, WIDE, 0, packed)
+    go(part(h, 0, 0, split), 2, 0, across, packed.at[:, 0:split])
+    go(chunk(h, 0), 4, 0, core, packed)
+    wait_for(part(1 - h, 0, split, WIDE), 3, 0)
+    along(1 - h, 0, split, WIDE, 1)
+    for away in order[1:]:
+        arrived(h, away, 0, WIDE, 0)
         along(h, away, 0, WIDE, 0)
         go(part(h, away, 0, split), 2, away % shards, across)
         go(chunk(h, away), 4, away % shards, core)
-        if away == 0:
-            wait_for(part(1 - h, 0, split, WIDE), 3, 0)
-        else:
-            wait_for(part(1 - h, away, split, WIDE), 1, away % shards)
+        arrived(1 - h, away, split, WIDE, 1)
         along(1 - h, away, split, WIDE, 1)
     for away in order:
         wait_for(part(1 - h, away, 0, split), 2, away % shards)
@@ -566,6 +579,7 @@
         for kind, half in ((4, h), (5, 1 - h)):
             ref = out.at[1 - p, half, ring_shard(r - away)]
             wait_for(ref, kind, away % shards)
+    own.wait()
     for copy in started:
         copy.wait_send()
 
@@ -612,10 +626,12 @@
     def own_part(half, away):
         return dw.at[half, ring_shard(r + away)]
 
-    ways = [(after, forward_hops, 1, 0), (before, back_hops, -1, forward_hops)]
+    mid = COLS // 2
+    ways = [(after, 1, 0, 0, mid), (before, -1, forward_hops, mid, COLS)]
     for half in range(2):
-        for device, hops, sign, first in ways:
-            go(own_part(half, sign * hops), slots.at[first, half], half, first, device)
+        for device, sign, first, a, b in ways:
+            src = dw.at[half, ring_shard(r + sign * forward_hops), :, a:b]
+            go(src, slots.at[first, half, :, a:b], half, first, device)
     go(small, smalls.at[h, ring_shard(r)], 2, 1, after)
     go(small, smalls.at[h, ring_shard(r)], 2, shards - 1, before)
     go(small, smalls.at[h, ring_shard(r)], 3, 0, across)
@@ -624,13 +640,18 @@
     smalls[h, ring_shard(r)] = small[...]
     for hop in range(forward_hops):
         for half in range(2):
-            for device, hops, sign, first in ways:
-                if hop < hops - 1:
+            for device, sign, first, a, b in ways:
+                if hop < forward_hops - 1:
                     at = first + hop
-                    wait_for(slots.at[at, half], half, at)
-                    moving[at, half] = (
-                        slots[at, half].astype(F32)
-                        + own_part(half, sign * (hops - 1 - hop))[...].astype(F32)
+                    own = own_part(half, sign * (forward_hops - 1 - hop))
+                    if hop == 0:
+                        wait_for(slots.at[at, half, :, a:b], half, at)
+                        moving[at, half] = own[...]
+                    else:
+                        a, b = 0, COLS
+                        wait_for(slots.at[at, half], half, at)
+                    moving[at, half, :, a:b] = (
+                        slots[at, half, :, a:b].astype(F32) + own[:, a:b].astype(F32)
                     ).astype(BF)
                     go(moving.at[at, half], slots.at[at + 1, half], half, at + 1, device)
         for away, device in ((hop + 1, after), (-hop - 1, before)):
@@ -641,7 +662,7 @@
                 if abs(away) < hops:
                     go(row, row, 2, (away + (1 if away > 0 else -1)) % shards, device)
                 go(row, row, 3, away % shards, across)
-    ends = [forward_hops - 1, shards - 2]
+    ends = [forward_hops - 1, 2 * forward_hops - 1]
     for half in range(2):
         for at in ends:
             wait_for(slots.at[at, half], half, at)
@@ -689,8 +710,8 @@
             jax.ShapeDtypeStruct(grad.shape, BF),
         ),
         scratch_shapes=[
-            pltpu.VMEM((shards - 1, 2) + part, BF),
-            pltpu.VMEM((shards - 1, 2) + part, BF),
+            pltpu.VMEM((shards, 2) + part, BF),
+            pltpu.VMEM((shards, 2) + part, BF),
             pltpu.VMEM(part, BF),
             pltpu.VMEM(part, BF),
             pltpu.SemaphoreType.DMA((6, shards)),

time: 171 us -> 152 us (0.89)
  Pallas kernels: 143 us -> 124 us
    pallas_call x1, Pallas kernels: 65.3 us -> 50.9 us  [gather_weights(): pl.pallas_call(kernel, in_specs=[pl.BlockSpec(memory_space=pl.ANY)], out_...]
    pallas_call x1, Pallas kernels: 51.9 us -> 46.4 us  [exchange(): pl.pallas_call(kernel, in_specs=[vmem] * 4, out_specs=[vmem] * 5, out_sha...]
where the time goes in v3:
time: 152 us; the launch traced here: 151 us
  Pallas kernels  124 us (82%)
  local copies, waits for them, and re-layouts  19.5 us (13%)
  other arithmetic  6.8 us (4%)
    pallas_call x1, Pallas kernels, gather_weights(): pl.pallas_call(kernel, in_specs=[pl.BlockSpec(memory_space=pl.ANY)], out_...  50.9 us
    pallas_call x1, Pallas kernels, exchange(): pl.pallas_call(kernel, in_specs=[vmem] * 4, out_specs=[vmem] * 5, out_sha...  46.4 us
    pallas_call x1, Pallas kernels, run_blocks(): pl.pallas_call(kernel, grid_spec=pltpu.PrefetchScalarGridSpec(num_scalar_...  26.3 us
    unnamed x12, local copies, waits for them, and re-layouts  4.48 us

profile of v3, /device:TPU:0, one launch (start us, length us, event | category | flops | bytes accessed | tf_op | source)
XLA Modules:
  0.0 151.1 jit_solution(13832068943199351711)
XLA Ops:
  0.7 1.0 copy.41
  1.6 0.9 copy.33
  2.7 0.8 reshape.139
  3.5 0.7 reshape.140
  4.2 2.1 %concatenate.15 = bf16[528]{0:T(1024)(128)(2,1)S(1)} concatenate(bf16[288]{0:T(512)(128)(2,1)S(1)} %reshape.139, bf16[48]{0:T(256)(128)(2,1)S(1)} %reshape.140, bf16[48]{0:T(256)(128)(2,1)} %bitcast.96, bf16[96]{0:T(256)(128)(2,1)} %bitcast.97, bf16[48]{0:T(256)(128)(2,1)} %bitcast.98), dimensions={0} | concatenate | bytes 2112 | tf_op jit(solution)/shard_map/concatenate | solution.py:365
  6.4 1.8 %concatenate.16.refs_0_ = bf16[48,3584]{1,0:T(8,128)(2,1)} concatenate(bf16[48,576]{1,0:T(8,128)(2,1)S(1)} %reshape.138, bf16[48,192]{1,0:T(8,128)(2,1)} %bitcast.95, bf16[48,768]{1,0:T(8,128)(2,1)} %bitcast.91, bf16[48,768]{1,0:T(8,128)(2,1)} %bitcast.92, bf16[48,1152]{1,0:T(8,128)(2,1)S(1)} %constant_dynamic-slice_fusion.3, bf16[48,11]{1,0:T(8,128)(2,1)S(1)} %reshape.144, ...), dimensions={1} | concatenate | bytes 688128 | tf_op jit(solution)/shard_map/concatenate | solution.py:374
  8.2 50.9 %shard_map.228 = bf16[2,2,8,48,3584]{4,3,2,1,0:T(8,128)(2,1)} custom-call(bf16[48,3584]{1,0:T(8,128)(2,1)} %concatenate.16.refs_0_), custom_call_target="tpu_custom_call" | custom-call | tf_op jit(solution)/shard_map/pallas_call | solution.py:593
  59.1 1.0 slice_convert_fusion
  60.9 0.7 reshape.165.refs_6_
  61.7 0.7 reshape_squeeze.14.refs_7_
  63.1 0.7 reshape.148.refs_5_
  63.8 0.7 reshape.152.refs_8_
  65.7 26.3 %shard_map.229 = (bf16[1,256,384]{2,1,0:T(8,128)(2,1)}, f32[1,256,384]{2,1,0:T(8,128)}, bf16[2,384,2304]{2,1,0:T(8,128)(2,1)}, f32[1,1,6528]{2,1,0:T(1,128)}) custom-call(s32[2]{0:T(128)} %pad_add_fusion.refs_0_, bf16[2,256,384]{2,1,0:T(8,128)(2,1)} %refs_1_.1, f32[2,1,384]{2,1,0:T(1,128)} %reshape.162.refs_2_, f32[2,256,384]{2,1,0:T(8,128)} %refs_3_.1, ...), custom_call_target="tpu_custom_call" | custom-call | flops 12000000000 | bytes 16000000 | tf_op jit(solution)/shard_map/pallas_call | solution.py:285
  92.0 1.1 convert_element_type.14.refs_3_
  93.0 0.8 pad.4
  93.8 0.9 copy-done
  94.7 46.4 %shard_map.230 = (f32[48,2304]{1,0:T(8,128)S(1)}, f32[2,8,1,56,128]{4,3,2,1,0:T(8,128)S(1)}, f32[2,1,56,128]{3,2,1,0:T(8,128)S(1)}, bf16[1,256,384]{2,1,0:T(8,128)(2,1)S(1)}, bf16[1,256,384]{2,1,0:T(8,128)(2,1)S(1)}) custom-call(bf16[2,8,48,2304]{3,2,1,0:T(8,128)(2,1)} %bitcast.83, f32[1,56,128]{2,1,0:T(8,128)S(1)} %bitcast.80, ...), custom_call_target="tpu_custom_call" | custom-call | tf_op jit(solution)/shard_map/pallas_call | solution.py:701
  142.5 0.8 copy.38
  144.2 1.0 convert_select_fusion.1
  145.2 0.9 maximum_bitcast_fusion
  146.2 0.8 maximum_bitcast_fusion.1
  149.0 0.7 copy.39
  149.6 0.7 slice_bitcast_fusion
  150.4 0.7 slice_bitcast_fusion.2
  (49 shorter events, 7.1 us)
Async XLA Ops:
  0.6 64.5 %copy-start.2 = (bf16[2,384]{1,0:T(2,128)(2,1)S(1)}, bf16[2,384]{1,0:T(2,128)(2,1)}, u32[]{:S(2)}) copy-start(bf16[2,384]{1,0:T(2,128)(2,1)} %param.14) | copy-start | bytes 4612
  92.0 54.2 %copy-start.1 = (bf16[1,256,384]{2,1,0:T(8,128)(2,1)S(1)}, bf16[1,256,384]{2,1,0:T(8,128)(2,1)}, u32[]{:S(2)}) copy-start(bf16[1,256,384]{2,1,0:T(8,128)(2,1)} %get-tuple-element.22.refs_2_) | copy-start | bytes 589828
  93.8 0.9 copy-start
